TPU v7x, 32 devices: a whole 2x2x4 slice. The times are simulated.
32 devices in a mesh: rep: 2 (over x), exp: 2 (over core), tp: 8 (over z, y).
Axes of the slice: x: 2, y: 2, z: 4, core: 2. Of those that a mesh axis runs over, the one named last changes fastest.
Arguments:
- tokens: bfloat16 [128, 4096], P(('rep', 'exp', 'tp')), parts along dimension 0, may hold values from -6 to 6
- expert_ids: int32 [128, 2], P(('rep', 'exp', 'tp')), parts along dimension 0, may hold values from 0 to 3, all different within a row; in each aligned block of 4 rows (0 to 3, 4 to 7, ...) at most 4 rows name the same one
- gate_ints: int32 [128, 2], P(('rep', 'exp', 'tp')), parts along dimension 0, may hold values from 16 to 240, as said below
- gate_weight: bfloat16 [4, 4096, 14336], P('exp', None, 'tp'), may hold values from -0.09375 to 0.09375
- up_weight: bfloat16 [4, 4096, 14336], P('exp', None, 'tp'), may hold values from -0.09375 to 0.09375
- down_weight: bfloat16 [4, 14336, 4096], P('exp', 'tp'), may hold values from -0.046875 to 0.046875
Outputs:
- mixed: bfloat16 [128, 4096], P(('rep', 'exp', 'tp')), parts along dimension 0
There are 2 independent parts, one for each index of `rep`. A program takes and returns all parts, laid end to end along the dimension named above; an argument that names none is the same for every part. Nothing has to cross between parts.
Inputs may be any that keep to these rules, and one draw needn't show every extreme that they name: `expert_ids`: each row names two different experts. Among the 4 rows of one device an expert is named at most 4 times, and exactly that often on some device. `gate_ints`: the two entries of a row sum to 256.
All inputs are finite; a program needn't handle non-finite values.
Results may differ from a plain program's by a relative error of at most 0.0049.
Values may be sent and summed in bfloat16 or wider, within the bound.
No kernel may reach another device: no remote copies, remote signals or barrier semaphores. Data moves between devices by JAX's collectives and lax.ppermute only.
A program may use at most 128 MiB of HBM per device.

v0:
```python
import jax
import jax.numpy as jnp
from jax import lax
from jax.sharding import PartitionSpec as P


def body(tokens, expert_ids, gate_ints, gate_weight, up_weight, down_weight):
    tok_rows, width = tokens.shape
    local_experts = gate_weight.shape[0]
    groups = lax.axis_size("exp")
    experts_all = local_experts * groups
    columns = experts_all * tok_rows
    flat_ids = expert_ids.reshape(-1)
    onehot = (flat_ids[:, None] == jnp.arange(experts_all, dtype=jnp.int32)[None, :]).astype(
        jnp.int32
    )
    before = jnp.cumsum(onehot, axis=0) - onehot
    position = jnp.sum(before * onehot, axis=1)
    owner = flat_ids // local_experts
    local = flat_ids % local_experts
    send_index = flat_ids * tok_rows + position
    placing = (send_index[:, None] == jnp.arange(columns, dtype=jnp.int32)[None, :]).astype(
        jnp.float32
    )
    placing = placing.reshape(tok_rows, 2, columns).sum(axis=1).astype(jnp.bfloat16)
    outgoing = jnp.einsum("tm,td->md", placing, tokens, preferred_element_type=jnp.float32).astype(
        jnp.bfloat16
    )
    outgoing = outgoing.reshape(groups, local_experts, tok_rows, width)
    arrived = lax.all_to_all(outgoing, "exp", split_axis=0, concat_axis=2, tiled=True)
    arrived = arrived.reshape(local_experts, groups * tok_rows, width)
    piece = lax.all_gather(arrived, "tp", axis=1, tiled=True)
    gate = jnp.einsum("lrd,ldf->lrf", piece, gate_weight, preferred_element_type=jnp.float32)
    upper = jnp.einsum("lrd,ldf->lrf", piece, up_weight, preferred_element_type=jnp.float32)
    hidden = (jax.nn.silu(gate) * upper).astype(jnp.bfloat16)
    summed = lax.psum_scatter(
        jnp.einsum("lrf,lfd->rld", hidden, down_weight, preferred_element_type=jnp.float32),
        "tp",
        scatter_dimension=0,
        tiled=True,
    )
    summed = summed.reshape(groups, tok_rows, local_experts, width)
    back = lax.all_to_all(summed, "exp", split_axis=0, concat_axis=0, tiled=True)
    back_index = (owner * tok_rows + position) * local_experts + local
    gates = gate_ints.reshape(-1).astype(jnp.float32) / 256.0
    combine = jnp.where(
        back_index[:, None] == jnp.arange(columns, dtype=jnp.int32)[None, :], gates[:, None], 0.0
    )
    combine = combine.reshape(tok_rows, 2, columns).sum(axis=1)
    mixed = jnp.dot(
        combine,
        back.reshape(columns, width),
        precision=lax.Precision.HIGHEST,
        preferred_element_type=jnp.float32,
    ).astype(jnp.bfloat16)
    return mixed


def solution(mesh):
    return jax.shard_map(
        body,
        mesh=mesh,
        in_specs=(
            P(("rep", "exp", "tp"), None),
            P(("rep", "exp", "tp"), None),
            P(("rep", "exp", "tp"), None),
            P("exp", None, "tp"),
            P("exp", None, "tp"),
            P("exp", "tp", None),
        ),
        out_specs=P(("rep", "exp", "tp"), None),
        check_vma=False,
    )
```

profile of v0, /device:TPU:0, one launch (start us, length us, event | category | flops | bytes accessed | tf_op | source)
XLA Modules:
  0.0 170.7 jit_solution(12089231413821765125)
XLA Ops:
  6.5 0.8 copy.24
  7.3 0.1 eq.45
  7.4 0.2 reduce_window_sum.11
  7.6 0.1 reduce_sum.30
  7.7 0.1 copy.31
  7.8 0.1 convert_reduce_fusion
  7.9 0.2 convolution_convert_fusion
  8.1 0.1 reshape.100
  8.2 3.8 %all_to_all.20 = bf16[2,2,4,4096]{3,2,1,0:T(4,128)(2,1)S(1)} all-to-all(bf16[2,2,4,4096]{3,2,1,0:T(4,128)(2,1)S(1)} %reshape.100), channel_id=1, replica_groups=mesh['rep'=2,'exp'=2,'tp'=8] {'exp'}, dimensions={0} | all-to-all | bytes 262144 | tf_op jit(solution)/shard_map/all_to_all | solution.py:30
  12.1 0.7 reshape.101
  12.8 0.0 all-gather.2.cloned.1.call-update
  12.8 0.0 reduce-scatter.2.cloned.1.call-start
  12.8 43.0 %all-gather.2.cloned.1.call-done = bf16[2,64,4096]{2,1,0:T(8,128)(2,1)} async-done(((bf16[2,8,4096]{2,1,0:T(8,128)(2,1)}), bf16[2,64,4096]{2,1,0:T(8,128)(2,1)}) %all-gather.2.cloned.1.call-update) | async-done | bytes 1048592 | tf_op jit(solution)/shard_map/all_gather | solution.py:32
  55.8 12.2 %fusion.16 = f32[2,64,1792]{2,1,0:T(8,128)S(1)} fusion(bf16[2,64,4096]{2,1,0:T(8,128)(2,1)} %all-gather.2.cloned.1.call-done, bf16[2,4096,1792]{2,1,0:T(8,128)(2,1)} %param.9), kind=kOutput, calls=%fused_computation.34 | convolution fusion | flops 1879048192 | bytes 31326208 | tf_op jit(solution)/shard_map/lrd,ldf->lrf/dot_general | solution.py:33
  68.0 0.0 copy-start.3
  68.0 23.1 %convolution_bitcast_fusion = f32[64,2,4096]{2,0,1:T(8,128)} fusion(bf16[2,1792,4096]{2,1,0:T(8,128)(2,1)} %param.11, bf16[2,64,4096]{2,1,0:T(8,128)(2,1)S(1)} %copy-done.2, bf16[2,4096,1792]{2,1,0:T(8,128)(2,1)} %param.10, f32[2,64,1792]{2,1,0:T(8,128)S(1)} %fusion.16), kind=kOutput, calls=%fused_computation | convolution fusion | flops 3759472640 | bytes 62783488 | tf_op jit(solution)/shard_map/lrf,lfd->rld/dot_general | solution.py:37
  91.1 0.0 reduce-scatter.2.cloned.1.call-update
  91.1 0.1 copy.29
  91.2 0.1 select_reduce_fusion
  91.3 66.4 %reduce-scatter.2.cloned.1.call-done = f32[8,2,4096]{2,0,1:T(8,128)} async-done(((f32[64,2,4096]{2,0,1:T(8,128)}), f32[8,2,4096]{2,0,1:T(8,128)}) %reduce-scatter.2.cloned.1.call-update) | async-done | bytes 262160 | tf_op jit(solution)/shard_map/reduce_scatter | solution.py:36
  157.7 1.2 copy.34
  158.8 3.9 %all_to_all.21 = f32[2,4,2,4096]{3,2,1,0:T(2,128)S(1)} all-to-all(f32[2,4,2,4096]{3,2,1,0:T(2,128)S(1)} %bitcast.15), channel_id=1, replica_groups=mesh['rep'=2,'exp'=2,'tp'=8] {'exp'}, dimensions={0} | all-to-all | bytes 524288 | tf_op jit(solution)/shard_map/all_to_all | solution.py:43
  162.8 0.2 reshape.103
  163.0 0.9 convolution_convert_fusion.1
  (13 shorter events, 0.1 us)
Async XLA Ops:
  6.5 1.4 copy-start
  6.5 49.3 %all-gather.2.cloned.1.call-start = ((), (), s32[]{:S(2)}) async-start(), calls=%async_computation.3 | async-start | bytes 1179648 | tf_op jit(solution)/shard_map/all_gather | solution.py:32
  12.8 144.9 %reduce-scatter.2.cloned.1.call-start = ((), (), s32[]{:S(2)}) async-start(), calls=%async_computation.4 | async-start | bytes 2359296 | tf_op jit(solution)/shard_map/reduce_scatter | solution.py:36
  55.8 12.2 %copy-start.2 = (bf16[2,64,4096]{2,1,0:T(8,128)(2,1)S(1)}, bf16[2,64,4096]{2,1,0:T(8,128)(2,1)}, u32[]{:S(2)}) copy-start(bf16[2,64,4096]{2,1,0:T(8,128)(2,1)} %all-gather.2.cloned.1.call-done) | copy-start | bytes 3145732
  68.0 23.2 %copy-start.3 = (s32[4,2]{0,1:T(2,128)S(1)}, s32[4,2]{0,1:T(2,128)}, u32[]{:S(2)}) copy-start(s32[4,2]{0,1:T(2,128)} %param.8) | copy-start | bytes 100
  68.0 95.8 %copy-start.1 = (bf16[4,4096]{1,0:T(4,128)(2,1)S(1)}, bf16[4,4096]{1,0:T(4,128)(2,1)}, u32[]{:S(2)}) copy-start(bf16[4,4096]{1,0:T(4,128)(2,1)} %param.6) | copy-start | bytes 98308
Sparse Core Ops, SparseCore 0:
  12.9 42.8 all-gather.1
  91.3 66.3 reduce-scatter.1
where the time goes:
time: 171 us
  waiting for transfers between devices  109 us (64%)
  matrix products  36.3 us (21%)
  between operations  13.5 us (8%)
  blocking collectives  7.78 us (5%)
  local copies, waits for them, and re-layouts  3.27 us (2%)
    reduce_scatter x1, waiting for transfers between devices, body(): lax.psum_scatter(jnp.einsum('lrf,lfd->rld', hidden, down_weight, preferre...  66.4 us
    all_gather x1, waiting for transfers between devices, body(): piece = lax.all_gather(arrived, 'tp', axis=1, tiled=True)  43 us
    dot_general x1, matrix products, body(): jnp.einsum('lrf,lfd->rld', hidden, down_weight, preferred_element_type=jn...  23.1 us
    dot_general x1, matrix products, body(): jnp.einsum('lrd,ldf->lrf', piece, gate_weight, preferred_element_type=jnp...  12.2 us
    all_to_all x1, blocking collectives, body(): lax.all_to_all(summed, 'exp', split_axis=0, concat_axis=0, tiled=True)  3.94 us
    all_to_all x1, blocking collectives, body(): lax.all_to_all(outgoing, 'exp', split_axis=0, concat_axis=2, tiled=True)  3.84 us
  transfers between devices with their start and end apart: 2, of which 2 were waited for; matrix products, arithmetic and copies ran while one was open for 0% of the time, Pallas kernels for 0%

commit v1 on v0

v1 whole, which is shorter than its diff:
```python
import functools

import jax
import jax.numpy as jnp
from jax import lax
from jax.experimental import pallas as pl
from jax.experimental.pallas import tpu as pltpu
from jax.sharding import PartitionSpec as P

AXES = ("rep", "exp", "tp")
LANES = 128


def partner(mesh_shape, rep_xor, exp_xor, tp_xor):
    reps, exps, tps = mesh_shape
    pairs = []
    for r in range(reps):
        for e in range(exps):
            for t in range(tps):
                here = (r * exps + e) * tps + t
                there = ((r ^ rep_xor) * exps + (e ^ exp_xor)) * tps + (t ^ tp_xor)
                pairs.append((here, there))
    return pairs


def exchange_rounds(mesh_shape):
    reps, _, tps = mesh_shape
    bits = [(0, 1 << b) for b in reversed(range(tps.bit_length() - 1))]
    bits += [(1 << b, 0) for b in range(reps.bit_length() - 1)]
    rounds = []
    for first in range(0, len(bits), 2):
        group = bits[first : first + 2]
        offsets = list(group)
        if len(group) == 2:
            offsets.append((group[0][0] ^ group[1][0], group[0][1] ^ group[1][1]))
        rounds.append(offsets)
    return rounds


def expert_kernel(
    width, experts_here, steps_in, steps_out, near, far, gate_w, up_w, down_w,
    keep, send, gate_v, up_v, down_v, gate_acc, up_acc, out_acc, sems,
):
    half = near.shape[0]
    rep = lax.axis_index("rep")
    first_local = rep * experts_here
    first_global = lax.axis_index("exp") * gate_w.shape[0] + first_local
    rows_in, rows_out = width // steps_in, gate_v.shape[1] // steps_out
    lane = lax.broadcasted_iota(jnp.int32, (half, LANES), 1)

    def in_copies(at, k):
        rows = pl.ds(k * rows_in, rows_in)
        return (
            pltpu.make_async_copy(gate_w.at[first_local + at, rows], gate_v.at[rows], sems.at[2 * k]),
            pltpu.make_async_copy(up_w.at[first_local + at, rows], up_v.at[rows], sems.at[2 * k + 1]),
        )

    def out_copy(at, k):
        rows = pl.ds(k * rows_out, rows_out)
        return pltpu.make_async_copy(
            down_w.at[first_local + at, rows], down_v.at[rows], sems.at[2 * steps_in + k]
        )

    for at in range(experts_here):
        ins = [in_copies(at, k) for k in range(steps_in)]
        outs = [out_copy(at, k) for k in range(steps_out)]
        for gate_copy, up_copy in ins:
            gate_copy.start()
            up_copy.start()
        for copy in outs:
            copy.start()
        for k, (gate_copy, up_copy) in enumerate(ins):
            cols = slice(k * rows_in, (k + 1) * rows_in)
            x = jnp.concatenate([near[:, cols], far[:, cols]], axis=0)
            gate_copy.wait()
            gate = jnp.dot(x, gate_v[cols, :], preferred_element_type=jnp.float32)
            gate_acc[...] = gate if k == 0 else gate_acc[...] + gate
            up_copy.wait()
            upper = jnp.dot(x, up_v[cols, :], preferred_element_type=jnp.float32)
            up_acc[...] = upper if k == 0 else up_acc[...] + upper
        gate = gate_acc[...]
        hidden = (gate / (1.0 + jnp.exp(-gate)) * up_acc[...]).astype(jnp.bfloat16)
        for k, copy in enumerate(outs):
            cols = slice(k * rows_out, (k + 1) * rows_out)
            copy.wait()
            term = jnp.dot(hidden[:, cols], down_v[cols, :], preferred_element_type=jnp.float32)
            out_acc[...] = term if k == 0 else out_acc[...] + term
        chosen = lane == first_global + at
        for rows, tokens, out in ((slice(0, half), near, keep), (slice(half, 2 * half), far, send)):
            tail = tokens[:, width:].astype(jnp.float32)
            weight = jnp.sum(jnp.where(chosen, tail, 0.0), axis=1, keepdims=True)
            scaled = weight * out_acc[rows, :]
            out[...] = (scaled if at == 0 else out[...] + scaled).astype(out.dtype)


def run_experts(near, far, gate_w, up_w, down_w, experts_here):
    half = near.shape[0]
    _, width, hidden = gate_w.shape
    steps_in = 8
    steps_out = hidden // 256 if hidden % 256 == 0 else 1
    any_spec = pl.BlockSpec(memory_space=pl.ANY)
    vmem_spec = pl.BlockSpec(memory_space=pltpu.VMEM)
    send_type = jnp.bfloat16 if experts_here == 1 else jnp.float32
    return pl.pallas_call(
        functools.partial(expert_kernel, width, experts_here, steps_in, steps_out),
        out_shape=(
            jax.ShapeDtypeStruct((half, width), jnp.float32),
            jax.ShapeDtypeStruct((half, width), send_type),
        ),
        in_specs=[vmem_spec, vmem_spec, any_spec, any_spec, any_spec],
        out_specs=(vmem_spec, vmem_spec),
        scratch_shapes=[
            pltpu.VMEM((width, hidden), jnp.bfloat16),
            pltpu.VMEM((width, hidden), jnp.bfloat16),
            pltpu.VMEM((hidden, width), jnp.bfloat16),
            pltpu.VMEM((2 * half, hidden), jnp.float32),
            pltpu.VMEM((2 * half, hidden), jnp.float32),
            pltpu.VMEM((2 * half, width), jnp.float32),
            pltpu.SemaphoreType.DMA((2 * steps_in + steps_out,)),
        ],
        compiler_params=pltpu.CompilerParams(vmem_limit_bytes=56 * 2**20),
    )(near, far, gate_w, up_w, down_w)


def body(mesh_shape, tokens, expert_ids, gate_ints, gate_weight, up_weight, down_weight):
    rows, width = tokens.shape
    experts_here = gate_weight.shape[0] // mesh_shape[0]

    def swap(x, rep_xor, exp_xor, tp_xor):
        return lax.ppermute(x, AXES, partner(mesh_shape, rep_xor, exp_xor, tp_xor))

    lanes = jnp.arange(LANES, dtype=jnp.int32)
    gates = gate_ints.astype(jnp.float32) / 256.0
    weights = jnp.sum(
        jnp.where(expert_ids[:, :, None] == lanes[None, None, :], gates[:, :, None], 0.0), axis=1
    )
    gathered = jnp.concatenate([tokens, weights.astype(jnp.bfloat16)], axis=1)
    rounds = exchange_rounds(mesh_shape)
    for offsets in rounds:
        gathered = jnp.concatenate(
            [gathered] + [swap(gathered, r, 0, t) for r, t in offsets], axis=0
        )
    far = swap(gathered, 0, 1, 0)
    keep, send = run_experts(gathered, far, gate_weight, up_weight, down_weight, experts_here)
    total = keep + swap(send, 0, 1, 0).astype(jnp.float32)
    for offsets in reversed(rounds):
        part = total.shape[0] // (len(offsets) + 1)
        pieces = [total[i * part : (i + 1) * part] for i in range(len(offsets) + 1)]
        total = pieces[0]
        for piece, (r, t) in zip(pieces[1:], offsets):
            total = total + swap(piece.astype(jnp.bfloat16), r, 0, t).astype(jnp.float32)
    return total.astype(jnp.bfloat16)


def solution(mesh):
    mesh_shape = tuple(mesh.shape[a] for a in AXES)
    return jax.shard_map(
        functools.partial(body, mesh_shape),
        mesh=mesh,
        in_specs=(
            P(AXES, None),
            P(AXES, None),
            P(AXES, None),
            P("exp", None, "tp"),
            P("exp", None, "tp"),
            P("exp", "tp", None),
        ),
        out_specs=P(AXES, None),
        check_vma=False,
    )
```

time: 171 us -> 63.6 us (0.37)
  waiting for transfers between devices: 109 us -> 22.7 us
  matrix products: 36.3 us -> 0 us
  starting transfers between devices: 0.04 us -> 17.5 us
  Pallas kernels: 0 us -> 16.6 us
  between operations: 13.5 us -> 0.08 us
  blocking collectives: 7.78 us -> 0 us
  other arithmetic: 0.4 us -> 5.12 us
  local copies, waits for them, and re-layouts: 3.27 us -> 1.26 us
    reduce_scatter x1 -> x0, waiting for transfers between devices: 66.4 us -> none  [body(): lax.psum_scatter(jnp.einsum('lrf,lfd->rld', hidden, down_weight, preferre...]
    all_gather x1 -> x0, waiting for transfers between devices: 43 us -> none  [body(): piece = lax.all_gather(arrived, 'tp', axis=1, tiled=True)]
    dot_general x4 -> x0, matrix products: 36.3 us -> none  [the longest x1 23.1 us: body(): jnp.einsum('lrf,lfd->rld', hidden, down_weight, preferred_element_type=jn...]
    ppermute x0 -> x14, waiting for transfers between devices: none -> 22.7 us  [swap(): return lax.ppermute(x, AXES, partner(mesh_shape, rep_xor, exp_xor, tp_xor))]
    ppermute x0 -> x14, starting transfers between devices: none -> 17.5 us  [swap(): return lax.ppermute(x, AXES, partner(mesh_shape, rep_xor, exp_xor, tp_xor))]
    pallas_call x0 -> x1, Pallas kernels: none -> 16.6 us  [run_experts(): pl.pallas_call(functools.partial(expert_kernel, width, experts_here, step...]
    all_to_all x2 -> x0, blocking collectives: 7.78 us -> none  [the longest x1 3.94 us: body(): lax.all_to_all(summed, 'exp', split_axis=0, concat_axis=0, tiled=True)]
    reshape x4 -> x0, local copies, waits for them, and re-layouts: 2.07 us -> none  [the longest x1 1.15 us: body(): summed = summed.reshape(groups, tok_rows, local_experts, width)]
  transfers between devices with their start and end apart: 2 -> 14, of which waited for: 2 -> 13; matrix products, arithmetic and copies ran while one was open for 0% -> 0% of each run, Pallas kernels for 0% -> 0%
where the time goes in v1:
time: 63.6 us; the launch traced here: 63.3 us
  waiting for transfers between devices  22.7 us (36%)
  starting transfers between devices  17.5 us (28%)
  Pallas kernels  16.6 us (26%)
  other arithmetic  5.12 us (8%)
  local copies, waits for them, and re-layouts  1.26 us (2%)
    ppermute x14, waiting for transfers between devices, swap(): return lax.ppermute(x, AXES, partner(mesh_shape, rep_xor, exp_xor, tp_xor))  22.7 us
    ppermute x14, starting transfers between devices, swap(): return lax.ppermute(x, AXES, partner(mesh_shape, rep_xor, exp_xor, tp_xor))  17.5 us
    pallas_call x1, Pallas kernels, run_experts(): pl.pallas_call(functools.partial(expert_kernel, width, experts_here, step...  16.6 us
    another operation x2, other arithmetic  1.42 us
  transfers between devices with their start and end apart: 14, of which 13 were waited for; matrix products, arithmetic and copies ran while one was open for 0% of the time, Pallas kernels for 0%

profile of v1, /device:TPU:0, one launch (start us, length us, event | category | flops | bytes accessed | tf_op | source)
XLA Modules:
  0.0 63.3 jit_solution(10358465784662926413)
XLA Ops:
  0.0 0.7 %convert_multiply_fusion = f32[4,2]{0,1:T(2,128)S(1)} fusion(s32[4,2]{0,1:T(2,128)} %param.8), kind=kLoop, calls=%fused_computation.12 | loop fusion | flops 16 | bytes 64 | tf_op jit(solution)/shard_map/div | solution.py:133
  0.7 0.8 %select_reduce_fusion = bf16[4,128]{1,0:T(4,128)(2,1)S(1)} fusion(f32[4,2]{0,1:T(2,128)S(1)} %convert_multiply_fusion, s32[4,2]{0,1:T(2,128)} %param.7), kind=kLoop, calls=%fused_computation.10 | loop fusion | flops 2560 | bytes 1088 | tf_op jit(solution)/shard_map/reduce_sum | solution.py:134
  1.4 0.8 %pad_maximum_fusion.1 = bf16[4,4224]{1,0:T(4,128)(2,1)S(1)} fusion(bf16[4,128]{1,0:T(4,128)(2,1)S(1)} %select_reduce_fusion, bf16[4,4096]{1,0:T(4,128)(2,1)} %param.6), kind=kLoop, calls=%fused_computation.9 | loop fusion | flops 67584 | bytes 67584 | tf_op jit(solution)/shard_map/concatenate | solution.py:137
  2.2 5.1 %collective-permute-start.2 = (bf16[4,4224]{1,0:T(4,128)(2,1)S(1)}, bf16[4,4224]{1,0:T(4,128)(2,1)S(1)}, u32[]{:S(2)}, u32[]{:S(2)}) collective-permute-start(bf16[4,4224]{1,0:T(4,128)(2,1)S(1)} %pad_maximum_fusion.1), channel_id=1, source_target_pairs={{0,6},{1,7},{2,4},{3,5},{4,2},{5,3},{6,0},{7,1},{8,14},{9,15},{10,... | collective-permute-start | bytes 101384 | tf_op jit(solution)/shard_map/ppermute | solution.py:130
  8.0 1.3 %collective-permute-done.2 = bf16[4,4224]{1,0:T(4,128)(2,1)S(1)} collective-permute-done((bf16[4,4224]{1,0:T(4,128)(2,1)S(1)}, bf16[4,4224]{1,0:T(4,128)(2,1)S(1)}, u32[]{:S(2)}, u32[]{:S(2)}) %collective-permute-start.2) | collective-permute-done | bytes 33824 | tf_op jit(solution)/shard_map/ppermute | solution.py:130
  9.2 2.0 %collective-permute-done.1 = bf16[4,4224]{1,0:T(4,128)(2,1)S(1)} collective-permute-done((bf16[4,4224]{1,0:T(4,128)(2,1)S(1)}, bf16[4,4224]{1,0:T(4,128)(2,1)S(1)}, u32[]{:S(2)}, u32[]{:S(2)}) %collective-permute-start.1) | collective-permute-done | bytes 33824 | tf_op jit(solution)/shard_map/ppermute | solution.py:130
  11.3 1.0 %collective-permute-done = bf16[4,4224]{1,0:T(4,128)(2,1)S(1)} collective-permute-done((bf16[4,4224]{1,0:T(4,128)(2,1)S(1)}, bf16[4,4224]{1,0:T(4,128)(2,1)S(1)}, u32[]{:S(2)}, u32[]{:S(2)}) %collective-permute-start) | collective-permute-done | bytes 33824 | tf_op jit(solution)/shard_map/ppermute | solution.py:130
  12.3 0.8 %pad_maximum_fusion = bf16[16,4224]{1,0:T(8,128)(2,1)S(1)} fusion(bf16[4,4224]{1,0:T(4,128)(2,1)S(1)} %collective-permute-done.2, bf16[4,4224]{1,0:T(4,128)(2,1)S(1)} %collective-permute-done.1, bf16[4,4224]{1,0:T(4,128)(2,1)S(1)} %collective-permute-done, bf16[4,128]{1,0:T(4,128)(2,1)S(1)} %select_reduce_fusion, bf16[4,4096]{1,0:T(4,128)(2,1)} %param.6), kind=kLoop, calls=%fused_computation.4 | loop fusion | flops 675840 | bytes 270336 | tf_op jit(solution)/shard_map/concatenate | solution.py:140
  13.1 2.5 %collective-permute-start.5 = (bf16[16,4224]{1,0:T(8,128)(2,1)S(1)}, bf16[16,4224]{1,0:T(8,128)(2,1)S(1)}, u32[]{:S(2)}, u32[]{:S(2)}) collective-permute-start(bf16[16,4224]{1,0:T(8,128)(2,1)S(1)} %pad_maximum_fusion), channel_id=1, source_target_pairs={{0,17},{1,16},{2,19},{3,18},{4,21},{5,20},{6,23},{7,22},{8,25},{9,... | collective-permute-start | bytes 405512 | tf_op jit(solution)/shard_map/ppermute | solution.py:130
  16.7 2.7 %collective-permute-done.5 = bf16[16,4224]{1,0:T(8,128)(2,1)S(1)} collective-permute-done((bf16[16,4224]{1,0:T(8,128)(2,1)S(1)}, bf16[16,4224]{1,0:T(8,128)(2,1)S(1)}, u32[]{:S(2)}, u32[]{:S(2)}) %collective-permute-start.5) | collective-permute-done | bytes 135200 | tf_op jit(solution)/shard_map/ppermute | solution.py:130
  19.4 1.4 %collective-permute-done.4 = bf16[16,4224]{1,0:T(8,128)(2,1)S(1)} collective-permute-done((bf16[16,4224]{1,0:T(8,128)(2,1)S(1)}, bf16[16,4224]{1,0:T(8,128)(2,1)S(1)}, u32[]{:S(2)}, u32[]{:S(2)}) %collective-permute-start.4) | collective-permute-done | bytes 135200 | tf_op jit(solution)/shard_map/ppermute | solution.py:130
  21.6 1.9 %collective-permute-done.6.far = bf16[64,4224]{1,0:T(8,128)(2,1)S(1)} collective-permute-done((bf16[64,4224]{1,0:T(8,128)(2,1)S(1)}, bf16[64,4224]{1,0:T(8,128)(2,1)S(1)}, u32[]{:S(2)}, u32[]{:S(2)}) %collective-permute-start.6) | collective-permute-done | bytes 540704 | tf_op jit(solution)/shard_map/ppermute | solution.py:130
  23.6 0.8 %copy-done.1 = bf16[64,4224]{1,0:T(8,128)(2,1)} copy-done((bf16[64,4224]{1,0:T(8,128)(2,1)}, bf16[64,4224]{1,0:T(8,128)(2,1)S(1)}, u32[]{:S(2)}) %copy-start.1) | copy-done | bytes 540696
  24.4 16.6 %shard_map.64 = (f32[64,4096]{1,0:T(8,128)}, bf16[64,4096]{1,0:T(8,128)(2,1)}) custom-call(bf16[64,4224]{1,0:T(8,128)(2,1)} %copy-done, bf16[64,4224]{1,0:T(8,128)(2,1)} %copy-done.1, bf16[2,4096,1792]{2,1,0:T(8,128)(2,1)} %gate_w.1, bf16[2,4096,1792]{2,1,0:T(8,128)(2,1)} %up_w.1, bf16[2,1792,4096]{2,1,0:T(8,128)(2,1)} %down_w.1), custom_call_target="tpu_custom_call" | custom-call | tf_op jit(solution)/shard_map/pallas_call | solution.py:104
  41.2 2.0 %collective-permute-done.7 = bf16[64,4096]{1,0:T(8,128)(2,1)S(1)} collective-permute-done((bf16[64,4096]{1,0:T(8,128)(2,1)}, bf16[64,4096]{1,0:T(8,128)(2,1)S(1)}, u32[]{:S(2)}, u32[]{:S(2)}) %collective-permute-start.7) | collective-permute-done | bytes 524320 | tf_op jit(solution)/shard_map/ppermute | solution.py:130
  43.2 1.3 %fusion.7 = (bf16[64,4096]{1,0:T(8,128)(2,1)S(1)}, f32[64,4096]{1,0:T(8,128)S(1)}) fusion(f32[64,4096]{1,0:T(8,128)} %get-tuple-element.7, bf16[64,4096]{1,0:T(8,128)(2,1)S(1)} %collective-permute-done.7), kind=kLoop, calls=%fused_computation.14 | loop fusion | flops 786432 | bytes 3145728 | tf_op jit(solution)/shard_map/convert.5
  44.6 1.2 %collective-permute-start.8 = (bf16[16,4096]{1,0:T(8,128)(2,1)S(1)}, bf16[16,4096]{1,0:T(8,128)(2,1)S(1)}, u32[]{:S(2)}, u32[]{:S(2)}) collective-permute-start(bf16[16,4096]{1,0:T(8,128)(2,1)S(1)} %get-tuple-element.13), channel_id=1, source_target_pairs={{0,1},{1,0},{2,3},{3,2},{4,5},{5,4},{6,7},{7,6},{8,9},{9,8},{10,11... | collective-permute-start | bytes 393224 | tf_op jit(solution)/shard_map/ppermute | solution.py:130
  45.8 2.0 %collective-permute-start.10 = (bf16[16,4096]{1,0:T(8,128)(2,1)S(1)}, bf16[16,4096]{1,0:T(8,128)(2,1)S(1)}, u32[]{:S(2)}, u32[]{:S(2)}) collective-permute-start(bf16[16,4096]{1,0:T(8,128)(2,1)S(1)} %get-tuple-element.14), channel_id=1, source_target_pairs={{0,17},{1,16},{2,19},{3,18},{4,21},{5,20},{6,23},{7,22},{8,25},{9,... | collective-permute-start | bytes 393224 | tf_op jit(solution)/shard_map/ppermute | solution.py:130
  48.2 4.8 %collective-permute-done.8 = bf16[16,4096]{1,0:T(8,128)(2,1)S(1)} collective-permute-done((bf16[16,4096]{1,0:T(8,128)(2,1)S(1)}, bf16[16,4096]{1,0:T(8,128)(2,1)S(1)}, u32[]{:S(2)}, u32[]{:S(2)}) %collective-permute-start.8) | collective-permute-done | bytes 131104 | tf_op jit(solution)/shard_map/ppermute | solution.py:130
  53.1 1.2 %collective-permute-done.9 = bf16[16,4096]{1,0:T(8,128)(2,1)S(1)} collective-permute-done((bf16[16,4096]{1,0:T(8,128)(2,1)S(1)}, bf16[16,4096]{1,0:T(8,128)(2,1)S(1)}, u32[]{:S(2)}, u32[]{:S(2)}) %collective-permute-start.9) | collective-permute-done | bytes 131104 | tf_op jit(solution)/shard_map/ppermute | solution.py:130
  54.4 0.7 %collective-permute-start.11 = (bf16[4,4096]{1,0:T(4,128)(2,1)S(1)}, bf16[4,4096]{1,0:T(4,128)(2,1)S(1)}, u32[]{:S(2)}, u32[]{:S(2)}) collective-permute-start(bf16[4,4096]{1,0:T(4,128)(2,1)S(1)} %get-tuple-element.16), channel_id=1, source_target_pairs={{0,4},{1,5},{2,6},{3,7},{4,0},{5,1},{6,2},{7,3},{8,12},{9,13},{10,... | collective-permute-start | bytes 98312 | tf_op jit(solution)/shard_map/ppermute | solution.py:130
  55.1 3.6 %collective-permute-start.13 = (bf16[4,4096]{1,0:T(4,128)(2,1)S(1)}, bf16[4,4096]{1,0:T(4,128)(2,1)S(1)}, u32[]{:S(2)}, u32[]{:S(2)}) collective-permute-start(bf16[4,4096]{1,0:T(4,128)(2,1)S(1)} %get-tuple-element.17), channel_id=1, source_target_pairs={{0,6},{1,7},{2,4},{3,5},{4,2},{5,3},{6,0},{7,1},{8,14},{9,15},{10,... | collective-permute-start | bytes 98312 | tf_op jit(solution)/shard_map/ppermute | solution.py:130
  59.4 1.6 %collective-permute-done.13 = bf16[4,4096]{1,0:T(4,128)(2,1)S(1)} collective-permute-done((bf16[4,4096]{1,0:T(4,128)(2,1)S(1)}, bf16[4,4096]{1,0:T(4,128)(2,1)S(1)}, u32[]{:S(2)}, u32[]{:S(2)}) %collective-permute-start.13) | collective-permute-done | bytes 32800 | tf_op jit(solution)/shard_map/ppermute | solution.py:130
  60.9 1.7 %collective-permute-done.12 = bf16[4,4096]{1,0:T(4,128)(2,1)S(1)} collective-permute-done((bf16[4,4096]{1,0:T(4,128)(2,1)S(1)}, bf16[4,4096]{1,0:T(4,128)(2,1)S(1)}, u32[]{:S(2)}, u32[]{:S(2)}) %collective-permute-start.12) | collective-permute-done | bytes 32800 | tf_op jit(solution)/shard_map/ppermute | solution.py:130
  (19 shorter events, 4.5 us)
Async XLA Ops:
  2.2 7.0 %collective-permute-start.2 = (bf16[4,4224]{1,0:T(4,128)(2,1)S(1)}, bf16[4,4224]{1,0:T(4,128)(2,1)S(1)}, u32[]{:S(2)}, u32[]{:S(2)}) collective-permute-start(bf16[4,4224]{1,0:T(4,128)(2,1)S(1)} %pad_maximum_fusion.1), channel_id=1, source_target_pairs={{0,6},{1,7},{2,4},{3,5},{4,2},{5,3},{6,0},{7,1},{8,14},{9,15},{10,... | collective-permute-start | bytes 101384 | tf_op jit(solution)/shard_map/ppermute | solution.py:130
  7.3 3.9 %collective-permute-start.1 = (bf16[4,4224]{1,0:T(4,128)(2,1)S(1)}, bf16[4,4224]{1,0:T(4,128)(2,1)S(1)}, u32[]{:S(2)}, u32[]{:S(2)}) collective-permute-start(bf16[4,4224]{1,0:T(4,128)(2,1)S(1)} %pad_maximum_fusion.1), channel_id=1, source_target_pairs={{0,2},{1,3},{2,0},{3,1},{4,6},{5,7},{6,4},{7,5},{8,10},{9,11},{10,... | collective-permute-start | bytes 101384 | tf_op jit(solution)/shard_map/ppermute | solution.py:130
  7.3 5.0 %collective-permute-start = (bf16[4,4224]{1,0:T(4,128)(2,1)S(1)}, bf16[4,4224]{1,0:T(4,128)(2,1)S(1)}, u32[]{:S(2)}, u32[]{:S(2)}) collective-permute-start(bf16[4,4224]{1,0:T(4,128)(2,1)S(1)} %pad_maximum_fusion.1), channel_id=1, source_target_pairs={{0,4},{1,5},{2,6},{3,7},{4,0},{5,1},{6,2},{7,3},{8,12},{9,13},{10,... | collective-permute-start | bytes 101384 | tf_op jit(solution)/shard_map/ppermute | solution.py:130
  13.1 6.3 %collective-permute-start.5 = (bf16[16,4224]{1,0:T(8,128)(2,1)S(1)}, bf16[16,4224]{1,0:T(8,128)(2,1)S(1)}, u32[]{:S(2)}, u32[]{:S(2)}) collective-permute-start(bf16[16,4224]{1,0:T(8,128)(2,1)S(1)} %pad_maximum_fusion), channel_id=1, source_target_pairs={{0,17},{1,16},{2,19},{3,18},{4,21},{5,20},{6,23},{7,22},{8,25},{9,... | collective-permute-start | bytes 405512 | tf_op jit(solution)/shard_map/ppermute | solution.py:130
  15.6 5.2 %collective-permute-start.4 = (bf16[16,4224]{1,0:T(8,128)(2,1)S(1)}, bf16[16,4224]{1,0:T(8,128)(2,1)S(1)}, u32[]{:S(2)}, u32[]{:S(2)}) collective-permute-start(bf16[16,4224]{1,0:T(8,128)(2,1)S(1)} %pad_maximum_fusion), channel_id=1, source_target_pairs={{0,16},{1,17},{2,18},{3,19},{4,20},{5,21},{6,22},{7,23},{8,24},{9,... | collective-permute-start | bytes 405512 | tf_op jit(solution)/shard_map/ppermute | solution.py:130
  16.2 5.0 %collective-permute-start.3 = (bf16[16,4224]{1,0:T(8,128)(2,1)S(1)}, bf16[16,4224]{1,0:T(8,128)(2,1)S(1)}, u32[]{:S(2)}, u32[]{:S(2)}) collective-permute-start(bf16[16,4224]{1,0:T(8,128)(2,1)S(1)} %pad_maximum_fusion), channel_id=1, source_target_pairs={{0,1},{1,0},{2,3},{3,2},{4,5},{5,4},{6,7},{7,6},{8,9},{9,8},{10,11... | collective-permute-start | bytes 405512 | tf_op jit(solution)/shard_map/ppermute | solution.py:130
  21.6 2.0 %copy-start = (bf16[64,4224]{1,0:T(8,128)(2,1)}, bf16[64,4224]{1,0:T(8,128)(2,1)S(1)}, u32[]{:S(2)}) copy-start(bf16[64,4224]{1,0:T(8,128)(2,1)S(1)} %concatenate.12.near) | copy-start | bytes 1622020
  21.6 2.0 %collective-permute-start.6 = (bf16[64,4224]{1,0:T(8,128)(2,1)S(1)}, bf16[64,4224]{1,0:T(8,128)(2,1)S(1)}, u32[]{:S(2)}, u32[]{:S(2)}) collective-permute-start(bf16[64,4224]{1,0:T(8,128)(2,1)S(1)} %concatenate.12.near), channel_id=1, source_target_pairs={{0,8},{1,9},{2,10},{3,11},{4,12},{5,13},{6,14},{7,15},{8,0},{9,1},... | collective-permute-start | bytes 1622024 | tf_op jit(solution)/shard_map/ppermute | solution.py:130
  23.6 0.8 %copy-start.1 = (bf16[64,4224]{1,0:T(8,128)(2,1)}, bf16[64,4224]{1,0:T(8,128)(2,1)S(1)}, u32[]{:S(2)}) copy-start(bf16[64,4224]{1,0:T(8,128)(2,1)S(1)} %collective-permute-done.6.far) | copy-start | bytes 1622020
  41.0 2.2 %collective-permute-start.7 = (bf16[64,4096]{1,0:T(8,128)(2,1)}, bf16[64,4096]{1,0:T(8,128)(2,1)S(1)}, u32[]{:S(2)}, u32[]{:S(2)}) collective-permute-start(bf16[64,4096]{1,0:T(8,128)(2,1)} %get-tuple-element.8), channel_id=1, source_target_pairs={{0,8},{1,9},{2,10},{3,11},{4,12},{5,13},{6,14},{7,15},{8,0},{9,1},... | collective-permute-start | bytes 1572872 | tf_op jit(solution)/shard_map/ppermute | solution.py:130
  44.6 8.4 %collective-permute-start.8 = (bf16[16,4096]{1,0:T(8,128)(2,1)S(1)}, bf16[16,4096]{1,0:T(8,128)(2,1)S(1)}, u32[]{:S(2)}, u32[]{:S(2)}) collective-permute-start(bf16[16,4096]{1,0:T(8,128)(2,1)S(1)} %get-tuple-element.13), channel_id=1, source_target_pairs={{0,1},{1,0},{2,3},{3,2},{4,5},{5,4},{6,7},{7,6},{8,9},{9,8},{10,11... | collective-permute-start | bytes 393224 | tf_op jit(solution)/shard_map/ppermute | solution.py:130
  45.8 7.3 %collective-permute-start.10 = (bf16[16,4096]{1,0:T(8,128)(2,1)S(1)}, bf16[16,4096]{1,0:T(8,128)(2,1)S(1)}, u32[]{:S(2)}, u32[]{:S(2)}) collective-permute-start(bf16[16,4096]{1,0:T(8,128)(2,1)S(1)} %get-tuple-element.14), channel_id=1, source_target_pairs={{0,17},{1,16},{2,19},{3,18},{4,21},{5,20},{6,23},{7,22},{8,25},{9,... | collective-permute-start | bytes 393224 | tf_op jit(solution)/shard_map/ppermute | solution.py:130
  47.8 6.4 %collective-permute-start.9 = (bf16[16,4096]{1,0:T(8,128)(2,1)S(1)}, bf16[16,4096]{1,0:T(8,128)(2,1)S(1)}, u32[]{:S(2)}, u32[]{:S(2)}) collective-permute-start(bf16[16,4096]{1,0:T(8,128)(2,1)S(1)} %get-tuple-element.15), channel_id=1, source_target_pairs={{0,16},{1,17},{2,18},{3,19},{4,20},{5,21},{6,22},{7,23},{8,24},{9,... | collective-permute-start | bytes 393224 | tf_op jit(solution)/shard_map/ppermute | solution.py:130
  54.4 5.0 %collective-permute-start.11 = (bf16[4,4096]{1,0:T(4,128)(2,1)S(1)}, bf16[4,4096]{1,0:T(4,128)(2,1)S(1)}, u32[]{:S(2)}, u32[]{:S(2)}) collective-permute-start(bf16[4,4096]{1,0:T(4,128)(2,1)S(1)} %get-tuple-element.16), channel_id=1, source_target_pairs={{0,4},{1,5},{2,6},{3,7},{4,0},{5,1},{6,2},{7,3},{8,12},{9,13},{10,... | collective-permute-start | bytes 98312 | tf_op jit(solution)/shard_map/ppermute | solution.py:130
  55.1 5.8 %collective-permute-start.13 = (bf16[4,4096]{1,0:T(4,128)(2,1)S(1)}, bf16[4,4096]{1,0:T(4,128)(2,1)S(1)}, u32[]{:S(2)}, u32[]{:S(2)}) collective-permute-start(bf16[4,4096]{1,0:T(4,128)(2,1)S(1)} %get-tuple-element.17), channel_id=1, source_target_pairs={{0,6},{1,7},{2,4},{3,5},{4,2},{5,3},{6,0},{7,1},{8,14},{9,15},{10,... | collective-permute-start | bytes 98312 | tf_op jit(solution)/shard_map/ppermute | solution.py:130
  58.7 3.9 %collective-permute-start.12 = (bf16[4,4096]{1,0:T(4,128)(2,1)S(1)}, bf16[4,4096]{1,0:T(4,128)(2,1)S(1)}, u32[]{:S(2)}, u32[]{:S(2)}) collective-permute-start(bf16[4,4096]{1,0:T(4,128)(2,1)S(1)} %get-tuple-element.18), channel_id=1, source_target_pairs={{0,2},{1,3},{2,0},{3,1},{4,6},{5,7},{6,4},{7,5},{8,10},{9,11},{10,... | collective-permute-start | bytes 98312 | tf_op jit(solution)/shard_map/ppermute | solution.py:130

commit v2 on v1

v2 whole, which is shorter than its diff:
```python
import functools

import jax
import jax.numpy as jnp
from jax import lax
from jax.experimental import pallas as pl
from jax.experimental.pallas import tpu as pltpu
from jax.sharding import PartitionSpec as P

AXES = ("rep", "exp", "tp")
LANES = 128
MIB = 2**20
EARLY_EIGHTHS = (2, 3, 1)
HBM = pl.BlockSpec(memory_space=pltpu.HBM)
VMEM = pl.BlockSpec(memory_space=pltpu.VMEM)
SMEM = pl.BlockSpec(memory_space=pltpu.SMEM)
ANY = pl.BlockSpec(memory_space=pl.ANY)


def partner(mesh_shape, rep_xor, exp_xor, tp_xor):
    reps, exps, tps = mesh_shape
    pairs = []
    for r in range(reps):
        for e in range(exps):
            for t in range(tps):
                here = (r * exps + e) * tps + t
                there = ((r ^ rep_xor) * exps + (e ^ exp_xor)) * tps + (t ^ tp_xor)
                pairs.append((here, there))
    return pairs


def exchange_rounds(mesh_shape):
    reps, _, tps = mesh_shape
    bits = [(0, 1 << b) for b in reversed(range(tps.bit_length() - 1))]
    bits += [(1 << b, 0) for b in range(reps.bit_length() - 1)]
    rounds = []
    for first in range(0, len(bits), 2):
        group = bits[first : first + 2]
        offsets = list(group)
        if len(group) == 2:
            offsets.append((group[0][0] ^ group[1][0], group[0][1] ^ group[1][1]))
        rounds.append(offsets)
    return rounds


def pack_kernel(ids, gates, tokens, packed):
    rows, width = tokens.shape
    packed[:, :width] = tokens[...]
    row = lax.broadcasted_iota(jnp.int32, (rows, LANES), 0)
    lane = lax.broadcasted_iota(jnp.int32, (rows, LANES), 1)
    weights = jnp.zeros((rows, LANES), jnp.float32)
    for t in range(rows):
        for k in range(ids.shape[0]):
            gate = gates[k, t].astype(jnp.float32) / 256.0
            weights += jnp.where((row == t) & (lane == ids[k, t]), gate, 0.0)
    packed[:, width:] = weights.astype(packed.dtype)


def pack(tokens, ids, gates):
    rows, width = tokens.shape
    return pl.pallas_call(
        pack_kernel,
        out_shape=jax.ShapeDtypeStruct((rows, width + LANES), tokens.dtype),
        in_specs=[SMEM, SMEM, VMEM],
        out_specs=VMEM,
        compiler_params=pltpu.CompilerParams(vmem_limit_bytes=2 * MIB),
    )(*(pltpu.with_memory_space_constraint(x, pltpu.HBM) for x in (ids.T, gates.T, tokens)))


def early_kernel(first, gate_w, up_w, after, gate_v, up_v, sems):
    del after
    rep = lax.axis_index("rep")
    rows = pl.ds(first, gate_v.shape[0])
    copies = [
        pltpu.make_async_copy(gate_w.at[rep, rows], gate_v, sems.at[0]),
        pltpu.make_async_copy(up_w.at[rep, rows], up_v, sems.at[1]),
    ]
    for copy in copies:
        copy.start()
    for copy in copies:
        copy.wait()


def load_early(gate_w, up_w, after, first, rows):
    hidden = gate_w.shape[2]
    size = rows * hidden * gate_w.dtype.itemsize
    return pl.pallas_call(
        functools.partial(early_kernel, first),
        out_shape=(pltpu.VMEM((rows, hidden), gate_w.dtype),) * 2,
        in_specs=[HBM, HBM, ANY],
        out_specs=(VMEM, VMEM),
        scratch_shapes=[pltpu.SemaphoreType.DMA((2,))],
        compiler_params=pltpu.CompilerParams(vmem_limit_bytes=MIB),
        cost_estimate=pl.CostEstimate(flops=0, bytes_accessed=4 * size, transcendentals=0),
    )(gate_w, up_w, after)


def expert_kernel(early, late_steps, down_steps, *refs):
    near, far, gate_w, up_w, down_w = refs[:5]
    loaded = refs[5 : 5 + 2 * early]
    keep, send, gate_v, up_v, down_v, gate_acc, up_acc, out_acc, sems = refs[5 + 2 * early :]
    half = near.shape[0]
    width = keep.shape[1]
    rep = lax.axis_index("rep")
    expert = lax.axis_index("exp") * gate_w.shape[0] + rep
    late_rows, hidden_width = gate_v.shape
    late_first = width - late_rows
    step_rows, down_rows = late_rows // late_steps, hidden_width // down_steps

    late, down = [], []
    for k in range(late_steps):
        there, here = pl.ds(late_first + k * step_rows, step_rows), pl.ds(k * step_rows, step_rows)
        late.append(
            (
                pltpu.make_async_copy(gate_w.at[rep, there], gate_v.at[here], sems.at[2 * k]),
                pltpu.make_async_copy(up_w.at[rep, there], up_v.at[here], sems.at[2 * k + 1]),
            )
        )
    for k in range(down_steps):
        rows = pl.ds(k * down_rows, down_rows)
        down.append(
            pltpu.make_async_copy(down_w.at[rep, rows], down_v.at[rows], sems.at[2 * late_steps + k])
        )
    for pair in late:
        for copy in pair:
            copy.start()
    for copy in down:
        copy.start()

    def tokens(first, rows):
        cols = slice(first, first + rows)
        return jnp.concatenate([near[:, cols], far[:, cols]], axis=0)

    first = 0
    for k in range(early):
        gate_p, up_p = loaded[2 * k], loaded[2 * k + 1]
        x = tokens(first, gate_p.shape[0])
        gate = jnp.dot(x, gate_p[...], preferred_element_type=jnp.float32)
        gate_acc[...] = gate if k == 0 else gate_acc[...] + gate
        upper = jnp.dot(x, up_p[...], preferred_element_type=jnp.float32)
        up_acc[...] = upper if k == 0 else up_acc[...] + upper
        first += gate_p.shape[0]
    for k, (gate_copy, up_copy) in enumerate(late):
        here = slice(k * step_rows, (k + 1) * step_rows)
        x = tokens(first, step_rows)
        gate_copy.wait()
        gate_acc[...] += jnp.dot(x, gate_v[here, :], preferred_element_type=jnp.float32)
        up_copy.wait()
        up_acc[...] += jnp.dot(x, up_v[here, :], preferred_element_type=jnp.float32)
        first += step_rows
    gate = gate_acc[...]
    hidden = (gate / (1.0 + jnp.exp(-gate)) * up_acc[...]).astype(jnp.bfloat16)
    for k, copy in enumerate(down):
        cols = slice(k * down_rows, (k + 1) * down_rows)
        copy.wait()
        term = jnp.dot(hidden[:, cols], down_v[cols, :], preferred_element_type=jnp.float32)
        out_acc[...] = term if k == 0 else out_acc[...] + term
    chosen = lax.broadcasted_iota(jnp.int32, (half, LANES), 1) == expert
    for rows, piece, out in ((slice(half, 2 * half), far, send), (slice(0, half), near, keep)):
        tail = piece[:, width:].astype(jnp.float32)
        weight = jnp.sum(jnp.where(chosen, tail, 0.0), axis=1, keepdims=True)
        out[...] = (weight * out_acc[rows, :]).astype(out.dtype)


def run_experts(near, far, loaded, gate_w, up_w, down_w):
    half = near.shape[0]
    _, width, hidden = gate_w.shape
    padded = -(-hidden // LANES) * LANES
    late_rows = width - sum(gate_p.shape[0] for gate_p, _ in loaded)
    late_steps = 2
    down_steps = hidden // 256 if hidden % 256 == 0 else 1
    scratch = 4 * late_rows * padded + 2 * hidden * width + 8 * half * (2 * padded + width)
    return pl.pallas_call(
        functools.partial(expert_kernel, len(loaded), late_steps, down_steps),
        out_shape=(
            jax.ShapeDtypeStruct((half, width), jnp.float32),
            jax.ShapeDtypeStruct((half, width), jnp.bfloat16),
        ),
        in_specs=[VMEM, VMEM, HBM, HBM, HBM] + [VMEM] * (2 * len(loaded)),
        out_specs=(VMEM, VMEM),
        scratch_shapes=[
            pltpu.VMEM((late_rows, hidden), jnp.bfloat16),
            pltpu.VMEM((late_rows, hidden), jnp.bfloat16),
            pltpu.VMEM((hidden, width), jnp.bfloat16),
            pltpu.VMEM((2 * half, hidden), jnp.float32),
            pltpu.VMEM((2 * half, hidden), jnp.float32),
            pltpu.VMEM((2 * half, width), jnp.float32),
            pltpu.SemaphoreType.DMA((2 * late_steps + down_steps,)),
        ],
        compiler_params=pltpu.CompilerParams(vmem_limit_bytes=scratch + 4 * MIB),
    )(near, far, gate_w, up_w, down_w, *(ref for pair in loaded for ref in pair))


def body(mesh_shape, tokens, expert_ids, gate_ints, gate_weight, up_weight, down_weight):
    width = tokens.shape[1]
    assert gate_weight.shape[0] == mesh_shape[0]
    gate_weight, up_weight, down_weight = (
        pltpu.with_memory_space_constraint(w, pltpu.HBM)
        for w in (gate_weight, up_weight, down_weight)
    )

    def swap(x, rep_xor, exp_xor, tp_xor):
        return lax.ppermute(x, AXES, partner(mesh_shape, rep_xor, exp_xor, tp_xor))

    gathered = pack(tokens, expert_ids, gate_ints)
    rounds = exchange_rounds(mesh_shape)
    shares = [e * width // 8 for e in EARLY_EIGHTHS]
    loaded, first = [], 0

    def load(rows):
        nonlocal first
        loaded.append(load_early(gate_weight, up_weight, gathered, first, rows))
        first += rows

    for at, offsets in enumerate(rounds):
        if at < len(shares) - 1:
            load(shares[at])
        gathered = jnp.concatenate(
            [gathered] + [swap(gathered, r, 0, t) for r, t in offsets], axis=0
        )
        if at < len(shares) - 1:
            gathered, loaded[-1] = lax.optimization_barrier((gathered, loaded[-1]))
    load(shares[-1])
    far = swap(gathered, 0, 1, 0)
    keep, send = run_experts(gathered, far, loaded, gate_weight, up_weight, down_weight)
    total = keep + swap(send, 0, 1, 0).astype(jnp.float32)
    for offsets in reversed(rounds):
        part = total.shape[0] // (len(offsets) + 1)
        pieces = [total[i * part : (i + 1) * part] for i in range(len(offsets) + 1)]
        total = pieces[0]
        for piece, (r, t) in zip(pieces[1:], offsets):
            total = total + swap(piece.astype(jnp.bfloat16), r, 0, t).astype(jnp.float32)
    return total.astype(jnp.bfloat16)


def solution(mesh):
    mesh_shape = tuple(mesh.shape[a] for a in AXES)
    return jax.shard_map(
        functools.partial(body, mesh_shape),
        mesh=mesh,
        in_specs=(
            P(AXES, None),
            P(AXES, None),
            P(AXES, None),
            P("exp", None, "tp"),
            P("exp", None, "tp"),
            P("exp", "tp", None),
        ),
        out_specs=P(AXES, None),
        check_vma=False,
    )
```

time: 63.6 us -> 52.4 us (0.82)
  waiting for transfers between devices: 22.7 us -> 13.1 us
  other arithmetic: 5.12 us -> 0.97 us
  Pallas kernels: 16.6 us -> 20.1 us
  local copies, waits for them, and re-layouts: 1.26 us -> 0.07 us
    ppermute x14, waiting for transfers between devices: 22.7 us -> 13.1 us  [swap(): return lax.ppermute(x, AXES, partner(mesh_shape, rep_xor, exp_xor, tp_xor))]
    pallas_call x1 -> x5, Pallas kernels: 16.6 us -> 20.1 us  [the longest x1 9.83 us: run_experts(): pl.pallas_call(functools.partial(expert_kernel, len(loaded), late_steps,...]
    another operation x2, other arithmetic: 1.42 us -> 0.19 us
    unnamed x4 -> x0, local copies, waits for them, and re-layouts: 0.83 us -> none
    concatenate x1 -> x0, other arithmetic: 0.77 us -> none  [body(): gathered = jnp.concatenate([tokens, weights.astype(jnp.bfloat16)], axis=1)]
    reduce_sum x1 -> x0, other arithmetic: 0.76 us -> none  [body(): jnp.sum(jnp.where(expert_ids[:, :, None] == lanes[None, None, :], gates[:...]
    concatenate x1 -> x2, other arithmetic: 0.84 us -> 0.13 us  [body(): jnp.concatenate([gathered] + [swap(gathered, r, 0, t) for r, t in offsets...]
    div x1 -> x0, other arithmetic: 0.68 us -> none  [body(): gates = gate_ints.astype(jnp.float32) / 256.0]
  transfers between devices with their start and end apart: 14 -> 14, of which waited for: 13 -> 9; matrix products, arithmetic and copies ran while one was open for 0% -> 0% of each run, Pallas kernels for 0% -> 18%
where the time goes in v2:
time: 52.4 us; the launch traced here: 52.2 us
  Pallas kernels  20.1 us (38%)
  starting transfers between devices  17.8 us (34%)
  waiting for transfers between devices  13.1 us (25%)
  other arithmetic  0.97 us (2%)
    ppermute x14, starting transfers between devices, swap(): return lax.ppermute(x, AXES, partner(mesh_shape, rep_xor, exp_xor, tp_xor))  17.8 us
    ppermute x14, waiting for transfers between devices, swap(): return lax.ppermute(x, AXES, partner(mesh_shape, rep_xor, exp_xor, tp_xor))  13.1 us
    pallas_call x1, Pallas kernels, run_experts(): pl.pallas_call(functools.partial(expert_kernel, len(loaded), late_steps,...  9.83 us
    pallas_call x3, Pallas kernels, load_early(): pl.pallas_call(functools.partial(early_kernel, first), out_shape=(pltpu.V...  9.47 us
  transfers between devices with their start and end apart: 14, of which 9 were waited for; matrix products, arithmetic and copies ran while one was open for 0% of the time, Pallas kernels for 18%

profile of v2, /device:TPU:0, one launch (start us, length us, event | category | flops | bytes accessed | tf_op | source)
XLA Modules:
  0.0 52.2 jit_solution(8863444454019643117)
XLA Ops:
  0.0 0.8 %shard_map.64.after = bf16[4,4224]{1,0:T(4,128)(2,1)S(1)} custom-call(s32[2,4]{1,0:T(2,128)} %bitcast.2, s32[2,4]{1,0:T(2,128)} %bitcast.3, bf16[4,4096]{1,0:T(4,128)(2,1)} %tokens.1), custom_call_target="tpu_custom_call" | custom-call | tf_op jit(solution)/shard_map/pallas_call | solution.py:61
  0.8 5.1 %collective-permute-start.2 = (bf16[4,4224]{1,0:T(4,128)(2,1)S(1)}, bf16[4,4224]{1,0:T(4,128)(2,1)S(1)}, u32[]{:S(2)}, u32[]{:S(2)}) collective-permute-start(bf16[4,4224]{1,0:T(4,128)(2,1)S(1)} %shard_map.64.after), channel_id=1, source_target_pairs={{0,6},{1,7},{2,4},{3,5},{4,2},{5,3},{6,0},{7,1},{8,14},{9,15},{10,... | collective-permute-start | bytes 101384 | tf_op jit(solution)/shard_map/ppermute | solution.py:203
  5.9 0.6 %collective-permute-start = (bf16[4,4224]{1,0:T(4,128)(2,1)S(1)}, bf16[4,4224]{1,0:T(4,128)(2,1)S(1)}, u32[]{:S(2)}, u32[]{:S(2)}) collective-permute-start(bf16[4,4224]{1,0:T(4,128)(2,1)S(1)} %shard_map.64.after), channel_id=1, source_target_pairs={{0,4},{1,5},{2,6},{3,7},{4,0},{5,1},{6,2},{7,3},{8,12},{9,13},{10,... | collective-permute-start | bytes 101384 | tf_op jit(solution)/shard_map/ppermute | solution.py:203
  6.5 3.2 %shard_map.65 = (bf16[1024,1792]{1,0:T(8,128)(2,1)S(1)}, bf16[1024,1792]{1,0:T(8,128)(2,1)S(1)}) custom-call(bf16[2,4096,1792]{2,1,0:T(8,128)(2,1)} %refs_2_.1, bf16[2,4096,1792]{2,1,0:T(8,128)(2,1)} %refs_3_.1, bf16[4,4224]{1,0:T(4,128)(2,1)S(1)} %shard_map.64.after), custom_call_target="tpu_custom_call" | custom-call | bytes 14680064 | tf_op jit(solution)/shard_map/pallas_call | solution.py:87
  9.8 1.0 %collective-permute-done = bf16[4,4224]{1,0:T(4,128)(2,1)S(1)} collective-permute-done((bf16[4,4224]{1,0:T(4,128)(2,1)S(1)}, bf16[4,4224]{1,0:T(4,128)(2,1)S(1)}, u32[]{:S(2)}, u32[]{:S(2)}) %collective-permute-start) | collective-permute-done | bytes 33824 | tf_op jit(solution)/shard_map/ppermute | solution.py:203
  10.9 2.5 %collective-permute-start.5 = (bf16[16,4224]{1,0:T(8,128)(2,1)S(1)}, bf16[16,4224]{1,0:T(8,128)(2,1)S(1)}, u32[]{:S(2)}, u32[]{:S(2)}) collective-permute-start(bf16[16,4224]{1,0:T(8,128)(2,1)S(1)} %pad_maximum_fusion.1.after), channel_id=1, source_target_pairs={{0,17},{1,16},{2,19},{3,18},{4,21},{5,20},{6,23},{7,22},{8,25},{9,... | collective-permute-start | bytes 405512 | tf_op jit(solution)/shard_map/ppermute | solution.py:203
  13.5 0.5 %collective-permute-start.4 = (bf16[16,4224]{1,0:T(8,128)(2,1)S(1)}, bf16[16,4224]{1,0:T(8,128)(2,1)S(1)}, u32[]{:S(2)}, u32[]{:S(2)}) collective-permute-start(bf16[16,4224]{1,0:T(8,128)(2,1)S(1)} %pad_maximum_fusion.1.after), channel_id=1, source_target_pairs={{0,16},{1,17},{2,18},{3,19},{4,20},{5,21},{6,22},{7,23},{8,24},{9,... | collective-permute-start | bytes 405512 | tf_op jit(solution)/shard_map/ppermute | solution.py:203
  14.0 0.5 collective-permute-start.3
  14.5 4.2 %shard_map.66 = (bf16[1536,1792]{1,0:T(8,128)(2,1)S(1)}, bf16[1536,1792]{1,0:T(8,128)(2,1)S(1)}) custom-call(bf16[2,4096,1792]{2,1,0:T(8,128)(2,1)} %refs_2_.1, bf16[2,4096,1792]{2,1,0:T(8,128)(2,1)} %refs_3_.1, bf16[16,4224]{1,0:T(8,128)(2,1)S(1)} %pad_maximum_fusion.1.after), custom_call_target="tpu_custom_call" | custom-call | bytes 22020096 | tf_op jit(solution)/shard_map/pallas_call | solution.py:87
  19.1 2.1 %shard_map.67 = (bf16[512,1792]{1,0:T(8,128)(2,1)S(1)}, bf16[512,1792]{1,0:T(8,128)(2,1)S(1)}) custom-call(bf16[2,4096,1792]{2,1,0:T(8,128)(2,1)} %refs_2_.1, bf16[2,4096,1792]{2,1,0:T(8,128)(2,1)} %refs_3_.1, bf16[64,4224]{1,0:T(8,128)(2,1)S(1)} %pad_maximum_fusion.after.refs_0_), custom_call_target="tpu_custom_call" | custom-call | bytes 7340032 | tf_op jit(solution)/shard_map/pallas_call | solution.py:87
  21.2 9.8 %shard_map.68 = (f32[64,4096]{1,0:T(8,128)S(1)}, bf16[64,4096]{1,0:T(8,128)(2,1)S(1)}) custom-call(bf16[64,4224]{1,0:T(8,128)(2,1)S(1)} %pad_maximum_fusion.after.refs_0_, bf16[64,4224]{1,0:T(8,128)(2,1)S(1)} %collective-permute-done.6.refs_1_, bf16[2,4096,1792]{2,1,0:T(8,128)(2,1)} %refs_2_.1, bf16[2,4096,1792]{2,1,0:T(8,128)(2,1)} %refs_3_.1, ...), custom_call_target="tpu_custom_call" | custom-call | tf_op jit(solution)/shard_map/pallas_call | solution.py:173
  31.1 0.6 %collective-permute-start.7 = (bf16[64,4096]{1,0:T(8,128)(2,1)S(1)}, bf16[64,4096]{1,0:T(8,128)(2,1)S(1)}, u32[]{:S(2)}, u32[]{:S(2)}) collective-permute-start(bf16[64,4096]{1,0:T(8,128)(2,1)S(1)} %get-tuple-element.32), channel_id=1, source_target_pairs={{0,8},{1,9},{2,10},{3,11},{4,12},{5,13},{6,14},{7,15},{8,0},{9,1},... | collective-permute-start | bytes 1572872 | tf_op jit(solution)/shard_map/ppermute | solution.py:203
  31.6 1.5 %collective-permute-done.7 = bf16[64,4096]{1,0:T(8,128)(2,1)S(1)} collective-permute-done((bf16[64,4096]{1,0:T(8,128)(2,1)S(1)}, bf16[64,4096]{1,0:T(8,128)(2,1)S(1)}, u32[]{:S(2)}, u32[]{:S(2)}) %collective-permute-start.7) | collective-permute-done | bytes 524320 | tf_op jit(solution)/shard_map/ppermute | solution.py:203
  33.3 1.3 %collective-permute-start.8 = (bf16[16,4096]{1,0:T(8,128)(2,1)S(1)}, bf16[16,4096]{1,0:T(8,128)(2,1)S(1)}, u32[]{:S(2)}, u32[]{:S(2)}) collective-permute-start(bf16[16,4096]{1,0:T(8,128)(2,1)S(1)} %get-tuple-element.37), channel_id=1, source_target_pairs={{0,1},{1,0},{2,3},{3,2},{4,5},{5,4},{6,7},{7,6},{8,9},{9,8},{10,11... | collective-permute-start | bytes 393224 | tf_op jit(solution)/shard_map/ppermute | solution.py:203
  34.7 1.7 %collective-permute-start.10 = (bf16[16,4096]{1,0:T(8,128)(2,1)S(1)}, bf16[16,4096]{1,0:T(8,128)(2,1)S(1)}, u32[]{:S(2)}, u32[]{:S(2)}) collective-permute-start(bf16[16,4096]{1,0:T(8,128)(2,1)S(1)} %get-tuple-element.38), channel_id=1, source_target_pairs={{0,17},{1,16},{2,19},{3,18},{4,21},{5,20},{6,23},{7,22},{8,25},{9,... | collective-permute-start | bytes 393224 | tf_op jit(solution)/shard_map/ppermute | solution.py:203
  36.4 0.5 %collective-permute-start.9 = (bf16[16,4096]{1,0:T(8,128)(2,1)S(1)}, bf16[16,4096]{1,0:T(8,128)(2,1)S(1)}, u32[]{:S(2)}, u32[]{:S(2)}) collective-permute-start(bf16[16,4096]{1,0:T(8,128)(2,1)S(1)} %get-tuple-element.39), channel_id=1, source_target_pairs={{0,16},{1,17},{2,18},{3,19},{4,20},{5,21},{6,22},{7,23},{8,24},{9,... | collective-permute-start | bytes 393224 | tf_op jit(solution)/shard_map/ppermute | solution.py:203
  36.9 5.1 %collective-permute-done.8 = bf16[16,4096]{1,0:T(8,128)(2,1)S(1)} collective-permute-done((bf16[16,4096]{1,0:T(8,128)(2,1)S(1)}, bf16[16,4096]{1,0:T(8,128)(2,1)S(1)}, u32[]{:S(2)}, u32[]{:S(2)}) %collective-permute-start.8) | collective-permute-done | bytes 131104 | tf_op jit(solution)/shard_map/ppermute | solution.py:203
  42.0 1.2 %collective-permute-done.9 = bf16[16,4096]{1,0:T(8,128)(2,1)S(1)} collective-permute-done((bf16[16,4096]{1,0:T(8,128)(2,1)S(1)}, bf16[16,4096]{1,0:T(8,128)(2,1)S(1)}, u32[]{:S(2)}, u32[]{:S(2)}) %collective-permute-start.9) | collective-permute-done | bytes 131104 | tf_op jit(solution)/shard_map/ppermute | solution.py:203
  43.3 1.9 %collective-permute-start.11 = (bf16[4,4096]{1,0:T(4,128)(2,1)S(1)}, bf16[4,4096]{1,0:T(4,128)(2,1)S(1)}, u32[]{:S(2)}, u32[]{:S(2)}) collective-permute-start(bf16[4,4096]{1,0:T(4,128)(2,1)S(1)} %get-tuple-element.40), channel_id=1, source_target_pairs={{0,4},{1,5},{2,6},{3,7},{4,0},{5,1},{6,2},{7,3},{8,12},{9,13},{10,... | collective-permute-start | bytes 98312 | tf_op jit(solution)/shard_map/ppermute | solution.py:203
  45.2 2.4 %collective-permute-start.13 = (bf16[4,4096]{1,0:T(4,128)(2,1)S(1)}, bf16[4,4096]{1,0:T(4,128)(2,1)S(1)}, u32[]{:S(2)}, u32[]{:S(2)}) collective-permute-start(bf16[4,4096]{1,0:T(4,128)(2,1)S(1)} %get-tuple-element.41), channel_id=1, source_target_pairs={{0,6},{1,7},{2,4},{3,5},{4,2},{5,3},{6,0},{7,1},{8,14},{9,15},{10,... | collective-permute-start | bytes 98312 | tf_op jit(solution)/shard_map/ppermute | solution.py:203
  47.7 0.8 %collective-permute-done.11 = bf16[4,4096]{1,0:T(4,128)(2,1)S(1)} collective-permute-done((bf16[4,4096]{1,0:T(4,128)(2,1)S(1)}, bf16[4,4096]{1,0:T(4,128)(2,1)S(1)}, u32[]{:S(2)}, u32[]{:S(2)}) %collective-permute-start.11) | collective-permute-done | bytes 32800 | tf_op jit(solution)/shard_map/ppermute | solution.py:203
  48.4 2.5 %collective-permute-done.13 = bf16[4,4096]{1,0:T(4,128)(2,1)S(1)} collective-permute-done((bf16[4,4096]{1,0:T(4,128)(2,1)S(1)}, bf16[4,4096]{1,0:T(4,128)(2,1)S(1)}, u32[]{:S(2)}, u32[]{:S(2)}) %collective-permute-start.13) | collective-permute-done | bytes 32800 | tf_op jit(solution)/shard_map/ppermute | solution.py:203
  50.9 0.6 %collective-permute-done.12 = bf16[4,4096]{1,0:T(4,128)(2,1)S(1)} collective-permute-done((bf16[4,4096]{1,0:T(4,128)(2,1)S(1)}, bf16[4,4096]{1,0:T(4,128)(2,1)S(1)}, u32[]{:S(2)}, u32[]{:S(2)}) %collective-permute-start.12) | collective-permute-done | bytes 32800 | tf_op jit(solution)/shard_map/ppermute | solution.py:203
  51.6 0.6 %fusion.4 = bf16[4,4096]{1,0:T(4,128)(2,1)} fusion(f32[16,4096]{1,0:T(8,128)S(1)} %get-tuple-element.34, bf16[4,4096]{1,0:T(4,128)(2,1)S(1)} %collective-permute-done.13, bf16[4,4096]{1,0:T(4,128)(2,1)S(1)} %collective-permute-done.12, bf16[4,4096]{1,0:T(4,128)(2,1)S(1)} %collective-permute-done.11), kind=kLoop, calls=%fused_computation.9 | loop fusion | flops 114688 | bytes 196608 | tf_op jit(solution)/shard_map/convert_element_type | solution.py:233
  (16 shorter events, 0.8 us)
Async XLA Ops:
  0.8 8.9 %collective-permute-start.2 = (bf16[4,4224]{1,0:T(4,128)(2,1)S(1)}, bf16[4,4224]{1,0:T(4,128)(2,1)S(1)}, u32[]{:S(2)}, u32[]{:S(2)}) collective-permute-start(bf16[4,4224]{1,0:T(4,128)(2,1)S(1)} %shard_map.64.after), channel_id=1, source_target_pairs={{0,6},{1,7},{2,4},{3,5},{4,2},{5,3},{6,0},{7,1},{8,14},{9,15},{10,... | collective-permute-start | bytes 101384 | tf_op jit(solution)/shard_map/ppermute | solution.py:203
  5.9 3.9 %collective-permute-start.1 = (bf16[4,4224]{1,0:T(4,128)(2,1)S(1)}, bf16[4,4224]{1,0:T(4,128)(2,1)S(1)}, u32[]{:S(2)}, u32[]{:S(2)}) collective-permute-start(bf16[4,4224]{1,0:T(4,128)(2,1)S(1)} %shard_map.64.after), channel_id=1, source_target_pairs={{0,2},{1,3},{2,0},{3,1},{4,6},{5,7},{6,4},{7,5},{8,10},{9,11},{10,... | collective-permute-start | bytes 101384 | tf_op jit(solution)/shard_map/ppermute | solution.py:203
  5.9 5.0 %collective-permute-start = (bf16[4,4224]{1,0:T(4,128)(2,1)S(1)}, bf16[4,4224]{1,0:T(4,128)(2,1)S(1)}, u32[]{:S(2)}, u32[]{:S(2)}) collective-permute-start(bf16[4,4224]{1,0:T(4,128)(2,1)S(1)} %shard_map.64.after), channel_id=1, source_target_pairs={{0,4},{1,5},{2,6},{3,7},{4,0},{5,1},{6,2},{7,3},{8,12},{9,13},{10,... | collective-permute-start | bytes 101384 | tf_op jit(solution)/shard_map/ppermute | solution.py:203
  10.9 7.8 %collective-permute-start.5 = (bf16[16,4224]{1,0:T(8,128)(2,1)S(1)}, bf16[16,4224]{1,0:T(8,128)(2,1)S(1)}, u32[]{:S(2)}, u32[]{:S(2)}) collective-permute-start(bf16[16,4224]{1,0:T(8,128)(2,1)S(1)} %pad_maximum_fusion.1.after), channel_id=1, source_target_pairs={{0,17},{1,16},{2,19},{3,18},{4,21},{5,20},{6,23},{7,22},{8,25},{9,... | collective-permute-start | bytes 405512 | tf_op jit(solution)/shard_map/ppermute | solution.py:203
  13.5 5.3 %collective-permute-start.4 = (bf16[16,4224]{1,0:T(8,128)(2,1)S(1)}, bf16[16,4224]{1,0:T(8,128)(2,1)S(1)}, u32[]{:S(2)}, u32[]{:S(2)}) collective-permute-start(bf16[16,4224]{1,0:T(8,128)(2,1)S(1)} %pad_maximum_fusion.1.after), channel_id=1, source_target_pairs={{0,16},{1,17},{2,18},{3,19},{4,20},{5,21},{6,22},{7,23},{8,24},{9,... | collective-permute-start | bytes 405512 | tf_op jit(solution)/shard_map/ppermute | solution.py:203
  14.0 5.0 %collective-permute-start.3 = (bf16[16,4224]{1,0:T(8,128)(2,1)S(1)}, bf16[16,4224]{1,0:T(8,128)(2,1)S(1)}, u32[]{:S(2)}, u32[]{:S(2)}) collective-permute-start(bf16[16,4224]{1,0:T(8,128)(2,1)S(1)} %pad_maximum_fusion.1.after), channel_id=1, source_target_pairs={{0,1},{1,0},{2,3},{3,2},{4,5},{5,4},{6,7},{7,6},{8,9},{9,8},{10,11... | collective-permute-start | bytes 405512 | tf_op jit(solution)/shard_map/ppermute | solution.py:203
  19.1 2.2 %collective-permute-start.6 = (bf16[64,4224]{1,0:T(8,128)(2,1)S(1)}, bf16[64,4224]{1,0:T(8,128)(2,1)S(1)}, u32[]{:S(2)}, u32[]{:S(2)}) collective-permute-start(bf16[64,4224]{1,0:T(8,128)(2,1)S(1)} %pad_maximum_fusion.after.refs_0_), channel_id=1, source_target_pairs={{0,8},{1,9},{2,10},{3,11},{4,12},{5,13},{6,14},{7,15},{8,0},{9,1},... | collective-permute-start | bytes 1622024 | tf_op jit(solution)/shard_map/ppermute | solution.py:203
  31.1 2.1 %collective-permute-start.7 = (bf16[64,4096]{1,0:T(8,128)(2,1)S(1)}, bf16[64,4096]{1,0:T(8,128)(2,1)S(1)}, u32[]{:S(2)}, u32[]{:S(2)}) collective-permute-start(bf16[64,4096]{1,0:T(8,128)(2,1)S(1)} %get-tuple-element.32), channel_id=1, source_target_pairs={{0,8},{1,9},{2,10},{3,11},{4,12},{5,13},{6,14},{7,15},{8,0},{9,1},... | collective-permute-start | bytes 1572872 | tf_op jit(solution)/shard_map/ppermute | solution.py:203
  33.3 8.6 %collective-permute-start.8 = (bf16[16,4096]{1,0:T(8,128)(2,1)S(1)}, bf16[16,4096]{1,0:T(8,128)(2,1)S(1)}, u32[]{:S(2)}, u32[]{:S(2)}) collective-permute-start(bf16[16,4096]{1,0:T(8,128)(2,1)S(1)} %get-tuple-element.37), channel_id=1, source_target_pairs={{0,1},{1,0},{2,3},{3,2},{4,5},{5,4},{6,7},{7,6},{8,9},{9,8},{10,11... | collective-permute-start | bytes 393224 | tf_op jit(solution)/shard_map/ppermute | solution.py:203
  34.7 7.3 %collective-permute-start.10 = (bf16[16,4096]{1,0:T(8,128)(2,1)S(1)}, bf16[16,4096]{1,0:T(8,128)(2,1)S(1)}, u32[]{:S(2)}, u32[]{:S(2)}) collective-permute-start(bf16[16,4096]{1,0:T(8,128)(2,1)S(1)} %get-tuple-element.38), channel_id=1, source_target_pairs={{0,17},{1,16},{2,19},{3,18},{4,21},{5,20},{6,23},{7,22},{8,25},{9,... | collective-permute-start | bytes 393224 | tf_op jit(solution)/shard_map/ppermute | solution.py:203
  36.4 6.8 %collective-permute-start.9 = (bf16[16,4096]{1,0:T(8,128)(2,1)S(1)}, bf16[16,4096]{1,0:T(8,128)(2,1)S(1)}, u32[]{:S(2)}, u32[]{:S(2)}) collective-permute-start(bf16[16,4096]{1,0:T(8,128)(2,1)S(1)} %get-tuple-element.39), channel_id=1, source_target_pairs={{0,16},{1,17},{2,18},{3,19},{4,20},{5,21},{6,22},{7,23},{8,24},{9,... | collective-permute-start | bytes 393224 | tf_op jit(solution)/shard_map/ppermute | solution.py:203
  43.3 5.1 %collective-permute-start.11 = (bf16[4,4096]{1,0:T(4,128)(2,1)S(1)}, bf16[4,4096]{1,0:T(4,128)(2,1)S(1)}, u32[]{:S(2)}, u32[]{:S(2)}) collective-permute-start(bf16[4,4096]{1,0:T(4,128)(2,1)S(1)} %get-tuple-element.40), channel_id=1, source_target_pairs={{0,4},{1,5},{2,6},{3,7},{4,0},{5,1},{6,2},{7,3},{8,12},{9,13},{10,... | collective-permute-start | bytes 98312 | tf_op jit(solution)/shard_map/ppermute | solution.py:203
  45.2 5.7 %collective-permute-start.13 = (bf16[4,4096]{1,0:T(4,128)(2,1)S(1)}, bf16[4,4096]{1,0:T(4,128)(2,1)S(1)}, u32[]{:S(2)}, u32[]{:S(2)}) collective-permute-start(bf16[4,4096]{1,0:T(4,128)(2,1)S(1)} %get-tuple-element.41), channel_id=1, source_target_pairs={{0,6},{1,7},{2,4},{3,5},{4,2},{5,3},{6,0},{7,1},{8,14},{9,15},{10,... | collective-permute-start | bytes 98312 | tf_op jit(solution)/shard_map/ppermute | solution.py:203
  47.7 3.9 %collective-permute-start.12 = (bf16[4,4096]{1,0:T(4,128)(2,1)S(1)}, bf16[4,4096]{1,0:T(4,128)(2,1)S(1)}, u32[]{:S(2)}, u32[]{:S(2)}) collective-permute-start(bf16[4,4096]{1,0:T(4,128)(2,1)S(1)} %get-tuple-element.42), channel_id=1, source_target_pairs={{0,2},{1,3},{2,0},{3,1},{4,6},{5,7},{6,4},{7,5},{8,10},{9,11},{10,... | collective-permute-start | bytes 98312 | tf_op jit(solution)/shard_map/ppermute | solution.py:203

commit v3 on v2

--- a/solution.py
+++ b/solution.py
@@ -10,7 +10,7 @@
 AXES = ("rep", "exp", "tp")
 LANES = 128
 MIB = 2**20
-EARLY_EIGHTHS = (2, 3, 1)
+EARLY_SHARES = (5, 7, 2)
 HBM = pl.BlockSpec(memory_space=pltpu.HBM)
 VMEM = pl.BlockSpec(memory_space=pltpu.VMEM)
 SMEM = pl.BlockSpec(memory_space=pltpu.SMEM)
@@ -98,7 +98,7 @@
 def expert_kernel(early, late_steps, down_steps, *refs):
     near, far, gate_w, up_w, down_w = refs[:5]
     loaded = refs[5 : 5 + 2 * early]
-    keep, send, gate_v, up_v, down_v, gate_acc, up_acc, out_acc, sems = refs[5 + 2 * early :]
+    keep, send, lead, gate_v, up_v, down_v, gate_acc, up_acc, out_acc, sems = refs[5 + 2 * early :]
     half = near.shape[0]
     width = keep.shape[1]
     rep = lax.axis_index("rep")
@@ -126,8 +126,20 @@
             copy.start()
     for copy in down:
         copy.start()
+    lead_cols = pl.ds(0, lead.shape[1])
+    last = 2 * late_steps + down_steps
+    leads = [
+        pltpu.make_async_copy(near.at[:, lead_cols], lead.at[pl.ds(0, half)], sems.at[last]),
+        pltpu.make_async_copy(far.at[:, lead_cols], lead.at[pl.ds(half, half)], sems.at[last + 1]),
+    ]
+    for copy in leads:
+        copy.start()
+    for copy in leads:
+        copy.wait()
 
     def tokens(first, rows):
+        if first == 0:
+            return lead[...]
         cols = slice(first, first + rows)
         return jnp.concatenate([near[:, cols], far[:, cols]], axis=0)
 
@@ -169,7 +181,8 @@
     late_rows = width - sum(gate_p.shape[0] for gate_p, _ in loaded)
     late_steps = 2
     down_steps = hidden // 256 if hidden % 256 == 0 else 1
-    scratch = 4 * late_rows * padded + 2 * hidden * width + 8 * half * (2 * padded + width)
+    lead_rows = loaded[0][0].shape[0]
+    scratch = 4 * half * lead_rows + 4 * late_rows * padded + 2 * hidden * width + 8 * half * (2 * padded + width)
     return pl.pallas_call(
         functools.partial(expert_kernel, len(loaded), late_steps, down_steps),
         out_shape=(
@@ -179,13 +192,14 @@
         in_specs=[VMEM, VMEM, HBM, HBM, HBM] + [VMEM] * (2 * len(loaded)),
         out_specs=(VMEM, VMEM),
         scratch_shapes=[
+            pltpu.VMEM((2 * half, lead_rows), jnp.bfloat16),
             pltpu.VMEM((late_rows, hidden), jnp.bfloat16),
             pltpu.VMEM((late_rows, hidden), jnp.bfloat16),
             pltpu.VMEM((hidden, width), jnp.bfloat16),
             pltpu.VMEM((2 * half, hidden), jnp.float32),
             pltpu.VMEM((2 * half, hidden), jnp.float32),
             pltpu.VMEM((2 * half, width), jnp.float32),
-            pltpu.SemaphoreType.DMA((2 * late_steps + down_steps,)),
+            pltpu.SemaphoreType.DMA((2 * late_steps + down_steps + 2,)),
         ],
         compiler_params=pltpu.CompilerParams(vmem_limit_bytes=scratch + 4 * MIB),
     )(near, far, gate_w, up_w, down_w, *(ref for pair in loaded for ref in pair))
@@ -204,7 +218,7 @@
 
     gathered = pack(tokens, expert_ids, gate_ints)
     rounds = exchange_rounds(mesh_shape)
-    shares = [e * width // 8 for e in EARLY_EIGHTHS]
+    shares = [e * width // 16 for e in EARLY_SHARES]
     loaded, first = [], 0
 
     def load(rows):

time: 52.4 us -> 49.9 us (0.952)
  Pallas kernels: 20.1 us -> 18.3 us
  waiting for transfers between devices: 13.1 us -> 12.4 us
    pallas_call x1, Pallas kernels: 9.83 us -> 7.06 us  [run_experts(): pl.pallas_call(functools.partial(expert_kernel, len(loaded), late_steps,...]
    pallas_call x3, Pallas kernels: 9.47 us -> 10.5 us  [load_early(): pl.pallas_call(functools.partial(early_kernel, first), out_shape=(pltpu.V...]
    ppermute x14, waiting for transfers between devices: 13.1 us -> 12.4 us  [swap(): return lax.ppermute(x, AXES, partner(mesh_shape, rep_xor, exp_xor, tp_xor))]
  transfers between devices with their start and end apart: 14 -> 14, of which waited for: 9 -> 8; matrix products, arithmetic and copies ran while one was open for 0% -> 0% of each run, Pallas kernels for 18% -> 21%
where the time goes in v3:
time: 49.9 us; the launch traced here: 49.7 us
  Pallas kernels  18.3 us (37%)
  starting transfers between devices  17.8 us (36%)
  waiting for transfers between devices  12.4 us (25%)
  other arithmetic  0.97 us (2%)
    ppermute x14, starting transfers between devices, swap(): return lax.ppermute(x, AXES, partner(mesh_shape, rep_xor, exp_xor, tp_xor))  17.8 us
    ppermute x14, waiting for transfers between devices, swap(): return lax.ppermute(x, AXES, partner(mesh_shape, rep_xor, exp_xor, tp_xor))  12.4 us
    pallas_call x3, Pallas kernels, load_early(): pl.pallas_call(functools.partial(early_kernel, first), out_shape=(pltpu.V...  10.5 us
    pallas_call x1, Pallas kernels, run_experts(): pl.pallas_call(functools.partial(expert_kernel, len(loaded), late_steps,...  7.06 us
  transfers between devices with their start and end apart: 14, of which 8 were waited for; matrix products, arithmetic and copies ran while one was open for 0% of the time, Pallas kernels for 21%

profile of v3, /device:TPU:0, one launch (start us, length us, event | category | flops | bytes accessed | tf_op | source)
XLA Modules:
  0.0 49.7 jit_solution(11087405602898171017)
XLA Ops:
  0.0 0.8 %shard_map.64.after = bf16[4,4224]{1,0:T(4,128)(2,1)S(1)} custom-call(s32[2,4]{1,0:T(2,128)} %bitcast.2, s32[2,4]{1,0:T(2,128)} %bitcast.3, bf16[4,4096]{1,0:T(4,128)(2,1)} %tokens.1), custom_call_target="tpu_custom_call" | custom-call | tf_op jit(solution)/shard_map/pallas_call | solution.py:61
  0.8 5.1 %collective-permute-start.2 = (bf16[4,4224]{1,0:T(4,128)(2,1)S(1)}, bf16[4,4224]{1,0:T(4,128)(2,1)S(1)}, u32[]{:S(2)}, u32[]{:S(2)}) collective-permute-start(bf16[4,4224]{1,0:T(4,128)(2,1)S(1)} %shard_map.64.after), channel_id=1, source_target_pairs={{0,6},{1,7},{2,4},{3,5},{4,2},{5,3},{6,0},{7,1},{8,14},{9,15},{10,... | collective-permute-start | bytes 101384 | tf_op jit(solution)/shard_map/ppermute | solution.py:217
  5.9 0.6 %collective-permute-start = (bf16[4,4224]{1,0:T(4,128)(2,1)S(1)}, bf16[4,4224]{1,0:T(4,128)(2,1)S(1)}, u32[]{:S(2)}, u32[]{:S(2)}) collective-permute-start(bf16[4,4224]{1,0:T(4,128)(2,1)S(1)} %shard_map.64.after), channel_id=1, source_target_pairs={{0,4},{1,5},{2,6},{3,7},{4,0},{5,1},{6,2},{7,3},{8,12},{9,13},{10,... | collective-permute-start | bytes 101384 | tf_op jit(solution)/shard_map/ppermute | solution.py:217
  6.5 3.7 %shard_map.65 = (bf16[1280,1792]{1,0:T(8,128)(2,1)S(1)}, bf16[1280,1792]{1,0:T(8,128)(2,1)S(1)}) custom-call(bf16[2,4096,1792]{2,1,0:T(8,128)(2,1)} %refs_2_.1, bf16[2,4096,1792]{2,1,0:T(8,128)(2,1)} %refs_3_.1, bf16[4,4224]{1,0:T(4,128)(2,1)S(1)} %shard_map.64.after), custom_call_target="tpu_custom_call" | custom-call | bytes 18350080 | tf_op jit(solution)/shard_map/pallas_call | solution.py:87
  10.3 0.6 %collective-permute-done = bf16[4,4224]{1,0:T(4,128)(2,1)S(1)} collective-permute-done((bf16[4,4224]{1,0:T(4,128)(2,1)S(1)}, bf16[4,4224]{1,0:T(4,128)(2,1)S(1)}, u32[]{:S(2)}, u32[]{:S(2)}) %collective-permute-start) | collective-permute-done | bytes 33824 | tf_op jit(solution)/shard_map/ppermute | solution.py:217
  10.9 2.5 %collective-permute-start.5 = (bf16[16,4224]{1,0:T(8,128)(2,1)S(1)}, bf16[16,4224]{1,0:T(8,128)(2,1)S(1)}, u32[]{:S(2)}, u32[]{:S(2)}) collective-permute-start(bf16[16,4224]{1,0:T(8,128)(2,1)S(1)} %pad_maximum_fusion.1.after), channel_id=1, source_target_pairs={{0,17},{1,16},{2,19},{3,18},{4,21},{5,20},{6,23},{7,22},{8,25},{9,... | collective-permute-start | bytes 405512 | tf_op jit(solution)/shard_map/ppermute | solution.py:217
  13.5 0.5 %collective-permute-start.4 = (bf16[16,4224]{1,0:T(8,128)(2,1)S(1)}, bf16[16,4224]{1,0:T(8,128)(2,1)S(1)}, u32[]{:S(2)}, u32[]{:S(2)}) collective-permute-start(bf16[16,4224]{1,0:T(8,128)(2,1)S(1)} %pad_maximum_fusion.1.after), channel_id=1, source_target_pairs={{0,16},{1,17},{2,18},{3,19},{4,20},{5,21},{6,22},{7,23},{8,24},{9,... | collective-permute-start | bytes 405512 | tf_op jit(solution)/shard_map/ppermute | solution.py:217
  14.0 0.5 %collective-permute-start.3 = (bf16[16,4224]{1,0:T(8,128)(2,1)S(1)}, bf16[16,4224]{1,0:T(8,128)(2,1)S(1)}, u32[]{:S(2)}, u32[]{:S(2)}) collective-permute-start(bf16[16,4224]{1,0:T(8,128)(2,1)S(1)} %pad_maximum_fusion.1.after), channel_id=1, source_target_pairs={{0,1},{1,0},{2,3},{3,2},{4,5},{5,4},{6,7},{7,6},{8,9},{9,8},{10,11... | collective-permute-start | bytes 405512 | tf_op jit(solution)/shard_map/ppermute | solution.py:217
  14.5 4.7 %shard_map.66 = (bf16[1792,1792]{1,0:T(8,128)(2,1)S(1)}, bf16[1792,1792]{1,0:T(8,128)(2,1)S(1)}) custom-call(bf16[2,4096,1792]{2,1,0:T(8,128)(2,1)} %refs_2_.1, bf16[2,4096,1792]{2,1,0:T(8,128)(2,1)} %refs_3_.1, bf16[16,4224]{1,0:T(8,128)(2,1)S(1)} %pad_maximum_fusion.1.after), custom_call_target="tpu_custom_call" | custom-call | bytes 25690112 | tf_op jit(solution)/shard_map/pallas_call | solution.py:87
  19.4 2.1 %shard_map.67 = (bf16[512,1792]{1,0:T(8,128)(2,1)S(1)}, bf16[512,1792]{1,0:T(8,128)(2,1)S(1)}) custom-call(bf16[2,4096,1792]{2,1,0:T(8,128)(2,1)} %refs_2_.1, bf16[2,4096,1792]{2,1,0:T(8,128)(2,1)} %refs_3_.1, bf16[64,4224]{1,0:T(8,128)(2,1)S(1)} %pad_maximum_fusion.after.refs_0_), custom_call_target="tpu_custom_call" | custom-call | bytes 7340032 | tf_op jit(solution)/shard_map/pallas_call | solution.py:87
  21.5 7.1 %shard_map.68 = (f32[64,4096]{1,0:T(8,128)S(1)}, bf16[64,4096]{1,0:T(8,128)(2,1)S(1)}) custom-call(bf16[64,4224]{1,0:T(8,128)(2,1)S(1)} %pad_maximum_fusion.after.refs_0_, bf16[64,4224]{1,0:T(8,128)(2,1)S(1)} %collective-permute-done.6.refs_1_, bf16[2,4096,1792]{2,1,0:T(8,128)(2,1)} %refs_2_.1, bf16[2,4096,1792]{2,1,0:T(8,128)(2,1)} %refs_3_.1, ...), custom_call_target="tpu_custom_call" | custom-call | tf_op jit(solution)/shard_map/pallas_call | solution.py:186
  28.5 0.5 %collective-permute-start.7 = (bf16[64,4096]{1,0:T(8,128)(2,1)S(1)}, bf16[64,4096]{1,0:T(8,128)(2,1)S(1)}, u32[]{:S(2)}, u32[]{:S(2)}) collective-permute-start(bf16[64,4096]{1,0:T(8,128)(2,1)S(1)} %get-tuple-element.32), channel_id=1, source_target_pairs={{0,8},{1,9},{2,10},{3,11},{4,12},{5,13},{6,14},{7,15},{8,0},{9,1},... | collective-permute-start | bytes 1572872 | tf_op jit(solution)/shard_map/ppermute | solution.py:217
  29.1 1.5 %collective-permute-done.7 = bf16[64,4096]{1,0:T(8,128)(2,1)S(1)} collective-permute-done((bf16[64,4096]{1,0:T(8,128)(2,1)S(1)}, bf16[64,4096]{1,0:T(8,128)(2,1)S(1)}, u32[]{:S(2)}, u32[]{:S(2)}) %collective-permute-start.7) | collective-permute-done | bytes 524320 | tf_op jit(solution)/shard_map/ppermute | solution.py:217
  30.8 1.6 %collective-permute-start.8 = (bf16[16,4096]{1,0:T(8,128)(2,1)S(1)}, bf16[16,4096]{1,0:T(8,128)(2,1)S(1)}, u32[]{:S(2)}, u32[]{:S(2)}) collective-permute-start(bf16[16,4096]{1,0:T(8,128)(2,1)S(1)} %get-tuple-element.37), channel_id=1, source_target_pairs={{0,1},{1,0},{2,3},{3,2},{4,5},{5,4},{6,7},{7,6},{8,9},{9,8},{10,11... | collective-permute-start | bytes 393224 | tf_op jit(solution)/shard_map/ppermute | solution.py:217
  32.4 1.4 %collective-permute-start.10 = (bf16[16,4096]{1,0:T(8,128)(2,1)S(1)}, bf16[16,4096]{1,0:T(8,128)(2,1)S(1)}, u32[]{:S(2)}, u32[]{:S(2)}) collective-permute-start(bf16[16,4096]{1,0:T(8,128)(2,1)S(1)} %get-tuple-element.38), channel_id=1, source_target_pairs={{0,17},{1,16},{2,19},{3,18},{4,21},{5,20},{6,23},{7,22},{8,25},{9,... | collective-permute-start | bytes 393224 | tf_op jit(solution)/shard_map/ppermute | solution.py:217
  33.8 0.5 %collective-permute-start.9 = (bf16[16,4096]{1,0:T(8,128)(2,1)S(1)}, bf16[16,4096]{1,0:T(8,128)(2,1)S(1)}, u32[]{:S(2)}, u32[]{:S(2)}) collective-permute-start(bf16[16,4096]{1,0:T(8,128)(2,1)S(1)} %get-tuple-element.39), channel_id=1, source_target_pairs={{0,16},{1,17},{2,18},{3,19},{4,20},{5,21},{6,22},{7,23},{8,24},{9,... | collective-permute-start | bytes 393224 | tf_op jit(solution)/shard_map/ppermute | solution.py:217
  34.3 4.8 %collective-permute-done.8 = bf16[16,4096]{1,0:T(8,128)(2,1)S(1)} collective-permute-done((bf16[16,4096]{1,0:T(8,128)(2,1)S(1)}, bf16[16,4096]{1,0:T(8,128)(2,1)S(1)}, u32[]{:S(2)}, u32[]{:S(2)}) %collective-permute-start.8) | collective-permute-done | bytes 131104 | tf_op jit(solution)/shard_map/ppermute | solution.py:217
  39.2 0.5 %collective-permute-done.10 = bf16[16,4096]{1,0:T(8,128)(2,1)S(1)} collective-permute-done((bf16[16,4096]{1,0:T(8,128)(2,1)S(1)}, bf16[16,4096]{1,0:T(8,128)(2,1)S(1)}, u32[]{:S(2)}, u32[]{:S(2)}) %collective-permute-start.10) | collective-permute-done | bytes 131104 | tf_op jit(solution)/shard_map/ppermute | solution.py:217
  39.7 1.0 %collective-permute-done.9 = bf16[16,4096]{1,0:T(8,128)(2,1)S(1)} collective-permute-done((bf16[16,4096]{1,0:T(8,128)(2,1)S(1)}, bf16[16,4096]{1,0:T(8,128)(2,1)S(1)}, u32[]{:S(2)}, u32[]{:S(2)}) %collective-permute-start.9) | collective-permute-done | bytes 131104 | tf_op jit(solution)/shard_map/ppermute | solution.py:217
  40.8 2.2 %collective-permute-start.11 = (bf16[4,4096]{1,0:T(4,128)(2,1)S(1)}, bf16[4,4096]{1,0:T(4,128)(2,1)S(1)}, u32[]{:S(2)}, u32[]{:S(2)}) collective-permute-start(bf16[4,4096]{1,0:T(4,128)(2,1)S(1)} %get-tuple-element.40), channel_id=1, source_target_pairs={{0,4},{1,5},{2,6},{3,7},{4,0},{5,1},{6,2},{7,3},{8,12},{9,13},{10,... | collective-permute-start | bytes 98312 | tf_op jit(solution)/shard_map/ppermute | solution.py:217
  43.0 2.1 %collective-permute-start.13 = (bf16[4,4096]{1,0:T(4,128)(2,1)S(1)}, bf16[4,4096]{1,0:T(4,128)(2,1)S(1)}, u32[]{:S(2)}, u32[]{:S(2)}) collective-permute-start(bf16[4,4096]{1,0:T(4,128)(2,1)S(1)} %get-tuple-element.41), channel_id=1, source_target_pairs={{0,6},{1,7},{2,4},{3,5},{4,2},{5,3},{6,0},{7,1},{8,14},{9,15},{10,... | collective-permute-start | bytes 98312 | tf_op jit(solution)/shard_map/ppermute | solution.py:217
  45.1 0.6 %collective-permute-done.11 = bf16[4,4096]{1,0:T(4,128)(2,1)S(1)} collective-permute-done((bf16[4,4096]{1,0:T(4,128)(2,1)S(1)}, bf16[4,4096]{1,0:T(4,128)(2,1)S(1)}, u32[]{:S(2)}, u32[]{:S(2)}) %collective-permute-start.11) | collective-permute-done | bytes 32800 | tf_op jit(solution)/shard_map/ppermute | solution.py:217
  45.6 3.1 %collective-permute-done.13 = bf16[4,4096]{1,0:T(4,128)(2,1)S(1)} collective-permute-done((bf16[4,4096]{1,0:T(4,128)(2,1)S(1)}, bf16[4,4096]{1,0:T(4,128)(2,1)S(1)}, u32[]{:S(2)}, u32[]{:S(2)}) %collective-permute-start.13) | collective-permute-done | bytes 32800 | tf_op jit(solution)/shard_map/ppermute | solution.py:217
  49.1 0.6 %fusion.4 = bf16[4,4096]{1,0:T(4,128)(2,1)} fusion(f32[16,4096]{1,0:T(8,128)S(1)} %get-tuple-element.34, bf16[4,4096]{1,0:T(4,128)(2,1)S(1)} %collective-permute-done.13, bf16[4,4096]{1,0:T(4,128)(2,1)S(1)} %collective-permute-done.12, bf16[4,4096]{1,0:T(4,128)(2,1)S(1)} %collective-permute-done.11), kind=kLoop, calls=%fused_computation.9 | loop fusion | flops 114688 | bytes 196608 | tf_op jit(solution)/shard_map/convert_element_type | solution.py:247
  (16 shorter events, 0.8 us)
Async XLA Ops:
  0.8 9.5 %collective-permute-start.2 = (bf16[4,4224]{1,0:T(4,128)(2,1)S(1)}, bf16[4,4224]{1,0:T(4,128)(2,1)S(1)}, u32[]{:S(2)}, u32[]{:S(2)}) collective-permute-start(bf16[4,4224]{1,0:T(4,128)(2,1)S(1)} %shard_map.64.after), channel_id=1, source_target_pairs={{0,6},{1,7},{2,4},{3,5},{4,2},{5,3},{6,0},{7,1},{8,14},{9,15},{10,... | collective-permute-start | bytes 101384 | tf_op jit(solution)/shard_map/ppermute | solution.py:217
  5.9 4.4 %collective-permute-start.1 = (bf16[4,4224]{1,0:T(4,128)(2,1)S(1)}, bf16[4,4224]{1,0:T(4,128)(2,1)S(1)}, u32[]{:S(2)}, u32[]{:S(2)}) collective-permute-start(bf16[4,4224]{1,0:T(4,128)(2,1)S(1)} %shard_map.64.after), channel_id=1, source_target_pairs={{0,2},{1,3},{2,0},{3,1},{4,6},{5,7},{6,4},{7,5},{8,10},{9,11},{10,... | collective-permute-start | bytes 101384 | tf_op jit(solution)/shard_map/ppermute | solution.py:217
  5.9 5.0 %collective-permute-start = (bf16[4,4224]{1,0:T(4,128)(2,1)S(1)}, bf16[4,4224]{1,0:T(4,128)(2,1)S(1)}, u32[]{:S(2)}, u32[]{:S(2)}) collective-permute-start(bf16[4,4224]{1,0:T(4,128)(2,1)S(1)} %shard_map.64.after), channel_id=1, source_target_pairs={{0,4},{1,5},{2,6},{3,7},{4,0},{5,1},{6,2},{7,3},{8,12},{9,13},{10,... | collective-permute-start | bytes 101384 | tf_op jit(solution)/shard_map/ppermute | solution.py:217
  10.9 8.3 %collective-permute-start.5 = (bf16[16,4224]{1,0:T(8,128)(2,1)S(1)}, bf16[16,4224]{1,0:T(8,128)(2,1)S(1)}, u32[]{:S(2)}, u32[]{:S(2)}) collective-permute-start(bf16[16,4224]{1,0:T(8,128)(2,1)S(1)} %pad_maximum_fusion.1.after), channel_id=1, source_target_pairs={{0,17},{1,16},{2,19},{3,18},{4,21},{5,20},{6,23},{7,22},{8,25},{9,... | collective-permute-start | bytes 405512 | tf_op jit(solution)/shard_map/ppermute | solution.py:217
  13.5 5.8 %collective-permute-start.4 = (bf16[16,4224]{1,0:T(8,128)(2,1)S(1)}, bf16[16,4224]{1,0:T(8,128)(2,1)S(1)}, u32[]{:S(2)}, u32[]{:S(2)}) collective-permute-start(bf16[16,4224]{1,0:T(8,128)(2,1)S(1)} %pad_maximum_fusion.1.after), channel_id=1, source_target_pairs={{0,16},{1,17},{2,18},{3,19},{4,20},{5,21},{6,22},{7,23},{8,24},{9,... | collective-permute-start | bytes 405512 | tf_op jit(solution)/shard_map/ppermute | solution.py:217
  14.0 5.2 %collective-permute-start.3 = (bf16[16,4224]{1,0:T(8,128)(2,1)S(1)}, bf16[16,4224]{1,0:T(8,128)(2,1)S(1)}, u32[]{:S(2)}, u32[]{:S(2)}) collective-permute-start(bf16[16,4224]{1,0:T(8,128)(2,1)S(1)} %pad_maximum_fusion.1.after), channel_id=1, source_target_pairs={{0,1},{1,0},{2,3},{3,2},{4,5},{5,4},{6,7},{7,6},{8,9},{9,8},{10,11... | collective-permute-start | bytes 405512 | tf_op jit(solution)/shard_map/ppermute | solution.py:217
  19.3 2.2 %collective-permute-start.6 = (bf16[64,4224]{1,0:T(8,128)(2,1)S(1)}, bf16[64,4224]{1,0:T(8,128)(2,1)S(1)}, u32[]{:S(2)}, u32[]{:S(2)}) collective-permute-start(bf16[64,4224]{1,0:T(8,128)(2,1)S(1)} %pad_maximum_fusion.after.refs_0_), channel_id=1, source_target_pairs={{0,8},{1,9},{2,10},{3,11},{4,12},{5,13},{6,14},{7,15},{8,0},{9,1},... | collective-permute-start | bytes 1622024 | tf_op jit(solution)/shard_map/ppermute | solution.py:217
  28.5 2.1 %collective-permute-start.7 = (bf16[64,4096]{1,0:T(8,128)(2,1)S(1)}, bf16[64,4096]{1,0:T(8,128)(2,1)S(1)}, u32[]{:S(2)}, u32[]{:S(2)}) collective-permute-start(bf16[64,4096]{1,0:T(8,128)(2,1)S(1)} %get-tuple-element.32), channel_id=1, source_target_pairs={{0,8},{1,9},{2,10},{3,11},{4,12},{5,13},{6,14},{7,15},{8,0},{9,1},... | collective-permute-start | bytes 1572872 | tf_op jit(solution)/shard_map/ppermute | solution.py:217
  30.8 8.4 %collective-permute-start.8 = (bf16[16,4096]{1,0:T(8,128)(2,1)S(1)}, bf16[16,4096]{1,0:T(8,128)(2,1)S(1)}, u32[]{:S(2)}, u32[]{:S(2)}) collective-permute-start(bf16[16,4096]{1,0:T(8,128)(2,1)S(1)} %get-tuple-element.37), channel_id=1, source_target_pairs={{0,1},{1,0},{2,3},{3,2},{4,5},{5,4},{6,7},{7,6},{8,9},{9,8},{10,11... | collective-permute-start | bytes 393224 | tf_op jit(solution)/shard_map/ppermute | solution.py:217
  32.4 7.3 %collective-permute-start.10 = (bf16[16,4096]{1,0:T(8,128)(2,1)S(1)}, bf16[16,4096]{1,0:T(8,128)(2,1)S(1)}, u32[]{:S(2)}, u32[]{:S(2)}) collective-permute-start(bf16[16,4096]{1,0:T(8,128)(2,1)S(1)} %get-tuple-element.38), channel_id=1, source_target_pairs={{0,17},{1,16},{2,19},{3,18},{4,21},{5,20},{6,23},{7,22},{8,25},{9,... | collective-permute-start | bytes 393224 | tf_op jit(solution)/shard_map/ppermute | solution.py:217
  33.8 6.8 %collective-permute-start.9 = (bf16[16,4096]{1,0:T(8,128)(2,1)S(1)}, bf16[16,4096]{1,0:T(8,128)(2,1)S(1)}, u32[]{:S(2)}, u32[]{:S(2)}) collective-permute-start(bf16[16,4096]{1,0:T(8,128)(2,1)S(1)} %get-tuple-element.39), channel_id=1, source_target_pairs={{0,16},{1,17},{2,18},{3,19},{4,20},{5,21},{6,22},{7,23},{8,24},{9,... | collective-permute-start | bytes 393224 | tf_op jit(solution)/shard_map/ppermute | solution.py:217
  40.8 4.9 %collective-permute-start.11 = (bf16[4,4096]{1,0:T(4,128)(2,1)S(1)}, bf16[4,4096]{1,0:T(4,128)(2,1)S(1)}, u32[]{:S(2)}, u32[]{:S(2)}) collective-permute-start(bf16[4,4096]{1,0:T(4,128)(2,1)S(1)} %get-tuple-element.40), channel_id=1, source_target_pairs={{0,4},{1,5},{2,6},{3,7},{4,0},{5,1},{6,2},{7,3},{8,12},{9,13},{10,... | collective-permute-start | bytes 98312 | tf_op jit(solution)/shard_map/ppermute | solution.py:217
  43.0 5.7 %collective-permute-start.13 = (bf16[4,4096]{1,0:T(4,128)(2,1)S(1)}, bf16[4,4096]{1,0:T(4,128)(2,1)S(1)}, u32[]{:S(2)}, u32[]{:S(2)}) collective-permute-start(bf16[4,4096]{1,0:T(4,128)(2,1)S(1)} %get-tuple-element.41), channel_id=1, source_target_pairs={{0,6},{1,7},{2,4},{3,5},{4,2},{5,3},{6,0},{7,1},{8,14},{9,15},{10,... | collective-permute-start | bytes 98312 | tf_op jit(solution)/shard_map/ppermute | solution.py:217
  45.1 4.0 %collective-permute-start.12 = (bf16[4,4096]{1,0:T(4,128)(2,1)S(1)}, bf16[4,4096]{1,0:T(4,128)(2,1)S(1)}, u32[]{:S(2)}, u32[]{:S(2)}) collective-permute-start(bf16[4,4096]{1,0:T(4,128)(2,1)S(1)} %get-tuple-element.42), channel_id=1, source_target_pairs={{0,2},{1,3},{2,0},{3,1},{4,6},{5,7},{6,4},{7,5},{8,10},{9,11},{10,... | collective-permute-start | bytes 98312 | tf_op jit(solution)/shard_map/ppermute | solution.py:217

commit v4 on v3

--- a/solution.py
+++ b/solution.py
@@ -36,10 +36,11 @@
     rounds = []
     for first in range(0, len(bits), 2):
         group = bits[first : first + 2]
-        offsets = list(group)
         if len(group) == 2:
-            offsets.append((group[0][0] ^ group[1][0], group[0][1] ^ group[1][1]))
-        rounds.append(offsets)
+            group.append((group[0][0] ^ group[1][0], group[0][1] ^ group[1][1]))
+            if first + 2 < len(bits):
+                group.reverse()
+        rounds.append(group)
     return rounds
 
 
@@ -242,7 +243,8 @@
         part = total.shape[0] // (len(offsets) + 1)
         pieces = [total[i * part : (i + 1) * part] for i in range(len(offsets) + 1)]
         total = pieces[0]
-        for piece, (r, t) in zip(pieces[1:], offsets):
+        moves = list(zip(pieces[1:], offsets))
+        for piece, (r, t) in moves if offsets is rounds[-1] else reversed(moves):
             total = total + swap(piece.astype(jnp.bfloat16), r, 0, t).astype(jnp.float32)
     return total.astype(jnp.bfloat16)
 

time: 49.9 us -> 49.2 us (0.986)
  starting transfers between devices: 17.8 us -> 17 us
    ppermute x14, starting transfers between devices: 17.8 us -> 17 us  [swap(): return lax.ppermute(x, AXES, partner(mesh_shape, rep_xor, exp_xor, tp_xor))]
where the time goes in v4:
time: 49.2 us; the launch traced here: 49 us
  Pallas kernels  18.3 us (37%)
  starting transfers between devices  17 us (35%)
  waiting for transfers between devices  12.5 us (25%)
  other arithmetic  0.97 us (2%)
    ppermute x14, starting transfers between devices, swap(): return lax.ppermute(x, AXES, partner(mesh_shape, rep_xor, exp_xor, tp_xor))  17 us
    ppermute x14, waiting for transfers between devices, swap(): return lax.ppermute(x, AXES, partner(mesh_shape, rep_xor, exp_xor, tp_xor))  12.5 us
    pallas_call x3, Pallas kernels, load_early(): pl.pallas_call(functools.partial(early_kernel, first), out_shape=(pltpu.V...  10.5 us
    pallas_call x1, Pallas kernels, run_experts(): pl.pallas_call(functools.partial(expert_kernel, len(loaded), late_steps,...  7.05 us
  transfers between devices with their start and end apart: 14, of which 8 were waited for; matrix products, arithmetic and copies ran while one was open for 0% of the time, Pallas kernels for 21%

profile of v4, /device:TPU:0, one launch (start us, length us, event | category | flops | bytes accessed | tf_op | source)
XLA Modules:
  0.0 49.0 jit_solution(9040972154596445017)
XLA Ops:
  0.0 0.8 %shard_map.64.after = bf16[4,4224]{1,0:T(4,128)(2,1)S(1)} custom-call(s32[2,4]{1,0:T(2,128)} %bitcast.2, s32[2,4]{1,0:T(2,128)} %bitcast.3, bf16[4,4096]{1,0:T(4,128)(2,1)} %tokens.1), custom_call_target="tpu_custom_call" | custom-call | tf_op jit(solution)/shard_map/pallas_call | solution.py:62
  0.8 4.1 %collective-permute-start.2 = (bf16[4,4224]{1,0:T(4,128)(2,1)S(1)}, bf16[4,4224]{1,0:T(4,128)(2,1)S(1)}, u32[]{:S(2)}, u32[]{:S(2)}) collective-permute-start(bf16[4,4224]{1,0:T(4,128)(2,1)S(1)} %shard_map.64.after), channel_id=1, source_target_pairs={{0,4},{1,5},{2,6},{3,7},{4,0},{5,1},{6,2},{7,3},{8,12},{9,13},{10,... | collective-permute-start | bytes 101384 | tf_op jit(solution)/shard_map/ppermute | solution.py:218
  4.9 1.6 %collective-permute-start.1 = (bf16[4,4224]{1,0:T(4,128)(2,1)S(1)}, bf16[4,4224]{1,0:T(4,128)(2,1)S(1)}, u32[]{:S(2)}, u32[]{:S(2)}) collective-permute-start(bf16[4,4224]{1,0:T(4,128)(2,1)S(1)} %shard_map.64.after), channel_id=1, source_target_pairs={{0,2},{1,3},{2,0},{3,1},{4,6},{5,7},{6,4},{7,5},{8,10},{9,11},{10,... | collective-permute-start | bytes 101384 | tf_op jit(solution)/shard_map/ppermute | solution.py:218
  6.5 3.7 %shard_map.65 = (bf16[1280,1792]{1,0:T(8,128)(2,1)S(1)}, bf16[1280,1792]{1,0:T(8,128)(2,1)S(1)}) custom-call(bf16[2,4096,1792]{2,1,0:T(8,128)(2,1)} %refs_2_.1, bf16[2,4096,1792]{2,1,0:T(8,128)(2,1)} %refs_3_.1, bf16[4,4224]{1,0:T(4,128)(2,1)S(1)} %shard_map.64.after), custom_call_target="tpu_custom_call" | custom-call | bytes 18350080 | tf_op jit(solution)/shard_map/pallas_call | solution.py:88
  10.2 2.0 %collective-permute-done = bf16[4,4224]{1,0:T(4,128)(2,1)S(1)} collective-permute-done((bf16[4,4224]{1,0:T(4,128)(2,1)S(1)}, bf16[4,4224]{1,0:T(4,128)(2,1)S(1)}, u32[]{:S(2)}, u32[]{:S(2)}) %collective-permute-start) | collective-permute-done | bytes 33824 | tf_op jit(solution)/shard_map/ppermute | solution.py:218
  12.3 2.5 %collective-permute-start.5 = (bf16[16,4224]{1,0:T(8,128)(2,1)S(1)}, bf16[16,4224]{1,0:T(8,128)(2,1)S(1)}, u32[]{:S(2)}, u32[]{:S(2)}) collective-permute-start(bf16[16,4224]{1,0:T(8,128)(2,1)S(1)} %pad_maximum_fusion.1.after), channel_id=1, source_target_pairs={{0,17},{1,16},{2,19},{3,18},{4,21},{5,20},{6,23},{7,22},{8,25},{9,... | collective-permute-start | bytes 405512 | tf_op jit(solution)/shard_map/ppermute | solution.py:218
  14.8 0.5 %collective-permute-start.4 = (bf16[16,4224]{1,0:T(8,128)(2,1)S(1)}, bf16[16,4224]{1,0:T(8,128)(2,1)S(1)}, u32[]{:S(2)}, u32[]{:S(2)}) collective-permute-start(bf16[16,4224]{1,0:T(8,128)(2,1)S(1)} %pad_maximum_fusion.1.after), channel_id=1, source_target_pairs={{0,16},{1,17},{2,18},{3,19},{4,20},{5,21},{6,22},{7,23},{8,24},{9,... | collective-permute-start | bytes 405512 | tf_op jit(solution)/shard_map/ppermute | solution.py:218
  15.3 0.5 %collective-permute-start.3 = (bf16[16,4224]{1,0:T(8,128)(2,1)S(1)}, bf16[16,4224]{1,0:T(8,128)(2,1)S(1)}, u32[]{:S(2)}, u32[]{:S(2)}) collective-permute-start(bf16[16,4224]{1,0:T(8,128)(2,1)S(1)} %pad_maximum_fusion.1.after), channel_id=1, source_target_pairs={{0,1},{1,0},{2,3},{3,2},{4,5},{5,4},{6,7},{7,6},{8,9},{9,8},{10,11... | collective-permute-start | bytes 405512 | tf_op jit(solution)/shard_map/ppermute | solution.py:218
  15.8 4.7 %shard_map.66 = (bf16[1792,1792]{1,0:T(8,128)(2,1)S(1)}, bf16[1792,1792]{1,0:T(8,128)(2,1)S(1)}) custom-call(bf16[2,4096,1792]{2,1,0:T(8,128)(2,1)} %refs_2_.1, bf16[2,4096,1792]{2,1,0:T(8,128)(2,1)} %refs_3_.1, bf16[16,4224]{1,0:T(8,128)(2,1)S(1)} %pad_maximum_fusion.1.after), custom_call_target="tpu_custom_call" | custom-call | bytes 25690112 | tf_op jit(solution)/shard_map/pallas_call | solution.py:88
  20.7 2.1 %shard_map.67 = (bf16[512,1792]{1,0:T(8,128)(2,1)S(1)}, bf16[512,1792]{1,0:T(8,128)(2,1)S(1)}) custom-call(bf16[2,4096,1792]{2,1,0:T(8,128)(2,1)} %refs_2_.1, bf16[2,4096,1792]{2,1,0:T(8,128)(2,1)} %refs_3_.1, bf16[64,4224]{1,0:T(8,128)(2,1)S(1)} %pad_maximum_fusion.after.refs_0_), custom_call_target="tpu_custom_call" | custom-call | bytes 7340032 | tf_op jit(solution)/shard_map/pallas_call | solution.py:88
  22.8 7.1 %shard_map.68 = (f32[64,4096]{1,0:T(8,128)S(1)}, bf16[64,4096]{1,0:T(8,128)(2,1)S(1)}) custom-call(bf16[64,4224]{1,0:T(8,128)(2,1)S(1)} %pad_maximum_fusion.after.refs_0_, bf16[64,4224]{1,0:T(8,128)(2,1)S(1)} %collective-permute-done.6.refs_1_, bf16[2,4096,1792]{2,1,0:T(8,128)(2,1)} %refs_2_.1, bf16[2,4096,1792]{2,1,0:T(8,128)(2,1)} %refs_3_.1, ...), custom_call_target="tpu_custom_call" | custom-call | tf_op jit(solution)/shard_map/pallas_call | solution.py:187
  29.9 0.6 %collective-permute-start.7 = (bf16[64,4096]{1,0:T(8,128)(2,1)S(1)}, bf16[64,4096]{1,0:T(8,128)(2,1)S(1)}, u32[]{:S(2)}, u32[]{:S(2)}) collective-permute-start(bf16[64,4096]{1,0:T(8,128)(2,1)S(1)} %get-tuple-element.32), channel_id=1, source_target_pairs={{0,8},{1,9},{2,10},{3,11},{4,12},{5,13},{6,14},{7,15},{8,0},{9,1},... | collective-permute-start | bytes 1572872 | tf_op jit(solution)/shard_map/ppermute | solution.py:218
  30.4 1.5 %collective-permute-done.7 = bf16[64,4096]{1,0:T(8,128)(2,1)S(1)} collective-permute-done((bf16[64,4096]{1,0:T(8,128)(2,1)S(1)}, bf16[64,4096]{1,0:T(8,128)(2,1)S(1)}, u32[]{:S(2)}, u32[]{:S(2)}) %collective-permute-start.7) | collective-permute-done | bytes 524320 | tf_op jit(solution)/shard_map/ppermute | solution.py:218
  32.1 1.6 %collective-permute-start.8 = (bf16[16,4096]{1,0:T(8,128)(2,1)S(1)}, bf16[16,4096]{1,0:T(8,128)(2,1)S(1)}, u32[]{:S(2)}, u32[]{:S(2)}) collective-permute-start(bf16[16,4096]{1,0:T(8,128)(2,1)S(1)} %get-tuple-element.37), channel_id=1, source_target_pairs={{0,1},{1,0},{2,3},{3,2},{4,5},{5,4},{6,7},{7,6},{8,9},{9,8},{10,11... | collective-permute-start | bytes 393224 | tf_op jit(solution)/shard_map/ppermute | solution.py:218
  33.7 1.4 %collective-permute-start.10 = (bf16[16,4096]{1,0:T(8,128)(2,1)S(1)}, bf16[16,4096]{1,0:T(8,128)(2,1)S(1)}, u32[]{:S(2)}, u32[]{:S(2)}) collective-permute-start(bf16[16,4096]{1,0:T(8,128)(2,1)S(1)} %get-tuple-element.38), channel_id=1, source_target_pairs={{0,17},{1,16},{2,19},{3,18},{4,21},{5,20},{6,23},{7,22},{8,25},{9,... | collective-permute-start | bytes 393224 | tf_op jit(solution)/shard_map/ppermute | solution.py:218
  35.1 0.5 %collective-permute-start.9 = (bf16[16,4096]{1,0:T(8,128)(2,1)S(1)}, bf16[16,4096]{1,0:T(8,128)(2,1)S(1)}, u32[]{:S(2)}, u32[]{:S(2)}) collective-permute-start(bf16[16,4096]{1,0:T(8,128)(2,1)S(1)} %get-tuple-element.39), channel_id=1, source_target_pairs={{0,16},{1,17},{2,18},{3,19},{4,20},{5,21},{6,22},{7,23},{8,24},{9,... | collective-permute-start | bytes 393224 | tf_op jit(solution)/shard_map/ppermute | solution.py:218
  35.7 4.8 %collective-permute-done.8 = bf16[16,4096]{1,0:T(8,128)(2,1)S(1)} collective-permute-done((bf16[16,4096]{1,0:T(8,128)(2,1)S(1)}, bf16[16,4096]{1,0:T(8,128)(2,1)S(1)}, u32[]{:S(2)}, u32[]{:S(2)}) %collective-permute-start.8) | collective-permute-done | bytes 131104 | tf_op jit(solution)/shard_map/ppermute | solution.py:218
  40.5 0.5 %collective-permute-done.10 = bf16[16,4096]{1,0:T(8,128)(2,1)S(1)} collective-permute-done((bf16[16,4096]{1,0:T(8,128)(2,1)S(1)}, bf16[16,4096]{1,0:T(8,128)(2,1)S(1)}, u32[]{:S(2)}, u32[]{:S(2)}) %collective-permute-start.10) | collective-permute-done | bytes 131104 | tf_op jit(solution)/shard_map/ppermute | solution.py:218
  41.0 1.0 %collective-permute-done.9 = bf16[16,4096]{1,0:T(8,128)(2,1)S(1)} collective-permute-done((bf16[16,4096]{1,0:T(8,128)(2,1)S(1)}, bf16[16,4096]{1,0:T(8,128)(2,1)S(1)}, u32[]{:S(2)}, u32[]{:S(2)}) %collective-permute-start.9) | collective-permute-done | bytes 131104 | tf_op jit(solution)/shard_map/ppermute | solution.py:218
  42.3 2.0 %collective-permute-start.13 = (bf16[4,4096]{1,0:T(4,128)(2,1)S(1)}, bf16[4,4096]{1,0:T(4,128)(2,1)S(1)}, u32[]{:S(2)}, u32[]{:S(2)}) collective-permute-start(bf16[4,4096]{1,0:T(4,128)(2,1)S(1)} %get-tuple-element.41), channel_id=1, source_target_pairs={{0,6},{1,7},{2,4},{3,5},{4,2},{5,3},{6,0},{7,1},{8,14},{9,15},{10,... | collective-permute-start | bytes 98312 | tf_op jit(solution)/shard_map/ppermute | solution.py:218
  44.3 1.4 %collective-permute-start.12 = (bf16[4,4096]{1,0:T(4,128)(2,1)S(1)}, bf16[4,4096]{1,0:T(4,128)(2,1)S(1)}, u32[]{:S(2)}, u32[]{:S(2)}) collective-permute-start(bf16[4,4096]{1,0:T(4,128)(2,1)S(1)} %get-tuple-element.42), channel_id=1, source_target_pairs={{0,2},{1,3},{2,0},{3,1},{4,6},{5,7},{6,4},{7,5},{8,10},{9,11},{10,... | collective-permute-start | bytes 98312 | tf_op jit(solution)/shard_map/ppermute | solution.py:218
  45.7 1.5 %collective-permute-done.11 = bf16[4,4096]{1,0:T(4,128)(2,1)S(1)} collective-permute-done((bf16[4,4096]{1,0:T(4,128)(2,1)S(1)}, bf16[4,4096]{1,0:T(4,128)(2,1)S(1)}, u32[]{:S(2)}, u32[]{:S(2)}) %collective-permute-start.11) | collective-permute-done | bytes 32800 | tf_op jit(solution)/shard_map/ppermute | solution.py:218
  47.1 0.9 %collective-permute-done.13 = bf16[4,4096]{1,0:T(4,128)(2,1)S(1)} collective-permute-done((bf16[4,4096]{1,0:T(4,128)(2,1)S(1)}, bf16[4,4096]{1,0:T(4,128)(2,1)S(1)}, u32[]{:S(2)}, u32[]{:S(2)}) %collective-permute-start.13) | collective-permute-done | bytes 32800 | tf_op jit(solution)/shard_map/ppermute | solution.py:218
  48.3 0.6 %fusion.4 = bf16[4,4096]{1,0:T(4,128)(2,1)} fusion(f32[16,4096]{1,0:T(8,128)S(1)} %get-tuple-element.34, bf16[4,4096]{1,0:T(4,128)(2,1)S(1)} %collective-permute-done.13, bf16[4,4096]{1,0:T(4,128)(2,1)S(1)} %collective-permute-done.12, bf16[4,4096]{1,0:T(4,128)(2,1)S(1)} %collective-permute-done.11), kind=kLoop, calls=%fused_computation.9 | loop fusion | flops 114688 | bytes 196608 | tf_op jit(solution)/shard_map/convert_element_type | solution.py:249
  (16 shorter events, 1.0 us)
Async XLA Ops:
  0.8 9.4 %collective-permute-start.2 = (bf16[4,4224]{1,0:T(4,128)(2,1)S(1)}, bf16[4,4224]{1,0:T(4,128)(2,1)S(1)}, u32[]{:S(2)}, u32[]{:S(2)}) collective-permute-start(bf16[4,4224]{1,0:T(4,128)(2,1)S(1)} %shard_map.64.after), channel_id=1, source_target_pairs={{0,4},{1,5},{2,6},{3,7},{4,0},{5,1},{6,2},{7,3},{8,12},{9,13},{10,... | collective-permute-start | bytes 101384 | tf_op jit(solution)/shard_map/ppermute | solution.py:218
  4.9 5.3 %collective-permute-start.1 = (bf16[4,4224]{1,0:T(4,128)(2,1)S(1)}, bf16[4,4224]{1,0:T(4,128)(2,1)S(1)}, u32[]{:S(2)}, u32[]{:S(2)}) collective-permute-start(bf16[4,4224]{1,0:T(4,128)(2,1)S(1)} %shard_map.64.after), channel_id=1, source_target_pairs={{0,2},{1,3},{2,0},{3,1},{4,6},{5,7},{6,4},{7,5},{8,10},{9,11},{10,... | collective-permute-start | bytes 101384 | tf_op jit(solution)/shard_map/ppermute | solution.py:218
  6.5 5.7 %collective-permute-start = (bf16[4,4224]{1,0:T(4,128)(2,1)S(1)}, bf16[4,4224]{1,0:T(4,128)(2,1)S(1)}, u32[]{:S(2)}, u32[]{:S(2)}) collective-permute-start(bf16[4,4224]{1,0:T(4,128)(2,1)S(1)} %shard_map.64.after), channel_id=1, source_target_pairs={{0,6},{1,7},{2,4},{3,5},{4,2},{5,3},{6,0},{7,1},{8,14},{9,15},{10,... | collective-permute-start | bytes 101384 | tf_op jit(solution)/shard_map/ppermute | solution.py:218
  12.3 8.3 %collective-permute-start.5 = (bf16[16,4224]{1,0:T(8,128)(2,1)S(1)}, bf16[16,4224]{1,0:T(8,128)(2,1)S(1)}, u32[]{:S(2)}, u32[]{:S(2)}) collective-permute-start(bf16[16,4224]{1,0:T(8,128)(2,1)S(1)} %pad_maximum_fusion.1.after), channel_id=1, source_target_pairs={{0,17},{1,16},{2,19},{3,18},{4,21},{5,20},{6,23},{7,22},{8,25},{9,... | collective-permute-start | bytes 405512 | tf_op jit(solution)/shard_map/ppermute | solution.py:218
  14.8 5.8 %collective-permute-start.4 = (bf16[16,4224]{1,0:T(8,128)(2,1)S(1)}, bf16[16,4224]{1,0:T(8,128)(2,1)S(1)}, u32[]{:S(2)}, u32[]{:S(2)}) collective-permute-start(bf16[16,4224]{1,0:T(8,128)(2,1)S(1)} %pad_maximum_fusion.1.after), channel_id=1, source_target_pairs={{0,16},{1,17},{2,18},{3,19},{4,20},{5,21},{6,22},{7,23},{8,24},{9,... | collective-permute-start | bytes 405512 | tf_op jit(solution)/shard_map/ppermute | solution.py:218
  15.3 5.2 %collective-permute-start.3 = (bf16[16,4224]{1,0:T(8,128)(2,1)S(1)}, bf16[16,4224]{1,0:T(8,128)(2,1)S(1)}, u32[]{:S(2)}, u32[]{:S(2)}) collective-permute-start(bf16[16,4224]{1,0:T(8,128)(2,1)S(1)} %pad_maximum_fusion.1.after), channel_id=1, source_target_pairs={{0,1},{1,0},{2,3},{3,2},{4,5},{5,4},{6,7},{7,6},{8,9},{9,8},{10,11... | collective-permute-start | bytes 405512 | tf_op jit(solution)/shard_map/ppermute | solution.py:218
  20.6 2.2 %collective-permute-start.6 = (bf16[64,4224]{1,0:T(8,128)(2,1)S(1)}, bf16[64,4224]{1,0:T(8,128)(2,1)S(1)}, u32[]{:S(2)}, u32[]{:S(2)}) collective-permute-start(bf16[64,4224]{1,0:T(8,128)(2,1)S(1)} %pad_maximum_fusion.after.refs_0_), channel_id=1, source_target_pairs={{0,8},{1,9},{2,10},{3,11},{4,12},{5,13},{6,14},{7,15},{8,0},{9,1},... | collective-permute-start | bytes 1622024 | tf_op jit(solution)/shard_map/ppermute | solution.py:218
  29.9 2.1 %collective-permute-start.7 = (bf16[64,4096]{1,0:T(8,128)(2,1)S(1)}, bf16[64,4096]{1,0:T(8,128)(2,1)S(1)}, u32[]{:S(2)}, u32[]{:S(2)}) collective-permute-start(bf16[64,4096]{1,0:T(8,128)(2,1)S(1)} %get-tuple-element.32), channel_id=1, source_target_pairs={{0,8},{1,9},{2,10},{3,11},{4,12},{5,13},{6,14},{7,15},{8,0},{9,1},... | collective-permute-start | bytes 1572872 | tf_op jit(solution)/shard_map/ppermute | solution.py:218
  32.1 8.4 %collective-permute-start.8 = (bf16[16,4096]{1,0:T(8,128)(2,1)S(1)}, bf16[16,4096]{1,0:T(8,128)(2,1)S(1)}, u32[]{:S(2)}, u32[]{:S(2)}) collective-permute-start(bf16[16,4096]{1,0:T(8,128)(2,1)S(1)} %get-tuple-element.37), channel_id=1, source_target_pairs={{0,1},{1,0},{2,3},{3,2},{4,5},{5,4},{6,7},{7,6},{8,9},{9,8},{10,11... | collective-permute-start | bytes 393224 | tf_op jit(solution)/shard_map/ppermute | solution.py:218
  33.7 7.3 %collective-permute-start.10 = (bf16[16,4096]{1,0:T(8,128)(2,1)S(1)}, bf16[16,4096]{1,0:T(8,128)(2,1)S(1)}, u32[]{:S(2)}, u32[]{:S(2)}) collective-permute-start(bf16[16,4096]{1,0:T(8,128)(2,1)S(1)} %get-tuple-element.38), channel_id=1, source_target_pairs={{0,17},{1,16},{2,19},{3,18},{4,21},{5,20},{6,23},{7,22},{8,25},{9,... | collective-permute-start | bytes 393224 | tf_op jit(solution)/shard_map/ppermute | solution.py:218
  35.1 6.8 %collective-permute-start.9 = (bf16[16,4096]{1,0:T(8,128)(2,1)S(1)}, bf16[16,4096]{1,0:T(8,128)(2,1)S(1)}, u32[]{:S(2)}, u32[]{:S(2)}) collective-permute-start(bf16[16,4096]{1,0:T(8,128)(2,1)S(1)} %get-tuple-element.39), channel_id=1, source_target_pairs={{0,16},{1,17},{2,18},{3,19},{4,20},{5,21},{6,22},{7,23},{8,24},{9,... | collective-permute-start | bytes 393224 | tf_op jit(solution)/shard_map/ppermute | solution.py:218
  42.1 5.0 %collective-permute-start.11 = (bf16[4,4096]{1,0:T(4,128)(2,1)S(1)}, bf16[4,4096]{1,0:T(4,128)(2,1)S(1)}, u32[]{:S(2)}, u32[]{:S(2)}) collective-permute-start(bf16[4,4096]{1,0:T(4,128)(2,1)S(1)} %get-tuple-element.40), channel_id=1, source_target_pairs={{0,4},{1,5},{2,6},{3,7},{4,0},{5,1},{6,2},{7,3},{8,12},{9,13},{10,... | collective-permute-start | bytes 98312 | tf_op jit(solution)/shard_map/ppermute | solution.py:218
  42.3 5.7 %collective-permute-start.13 = (bf16[4,4096]{1,0:T(4,128)(2,1)S(1)}, bf16[4,4096]{1,0:T(4,128)(2,1)S(1)}, u32[]{:S(2)}, u32[]{:S(2)}) collective-permute-start(bf16[4,4096]{1,0:T(4,128)(2,1)S(1)} %get-tuple-element.41), channel_id=1, source_target_pairs={{0,6},{1,7},{2,4},{3,5},{4,2},{5,3},{6,0},{7,1},{8,14},{9,15},{10,... | collective-permute-start | bytes 98312 | tf_op jit(solution)/shard_map/ppermute | solution.py:218
  44.3 4.1 %collective-permute-start.12 = (bf16[4,4096]{1,0:T(4,128)(2,1)S(1)}, bf16[4,4096]{1,0:T(4,128)(2,1)S(1)}, u32[]{:S(2)}, u32[]{:S(2)}) collective-permute-start(bf16[4,4096]{1,0:T(4,128)(2,1)S(1)} %get-tuple-element.42), channel_id=1, source_target_pairs={{0,2},{1,3},{2,0},{3,1},{4,6},{5,7},{6,4},{7,5},{8,10},{9,11},{10,... | collective-permute-start | bytes 98312 | tf_op jit(solution)/shard_map/ppermute | solution.py:218

commit v5 on v4

--- a/solution.py
+++ b/solution.py
@@ -17,11 +17,12 @@
 ANY = pl.BlockSpec(memory_space=pl.ANY)
 
 
-def partner(mesh_shape, rep_xor, exp_xor, tp_xor):
+def partner(mesh_shape, exp_xor, offsets):
     reps, exps, tps = mesh_shape
     pairs = []
     for r in range(reps):
         for e in range(exps):
+            rep_xor, tp_xor = offsets[e % 2]
             for t in range(tps):
                 here = (r * exps + e) * tps + t
                 there = ((r ^ rep_xor) * exps + (e ^ exp_xor)) * tps + (t ^ tp_xor)
@@ -40,7 +41,10 @@
             group.append((group[0][0] ^ group[1][0], group[0][1] ^ group[1][1]))
             if first + 2 < len(bits):
                 group.reverse()
-        rounds.append(group)
+        other = group
+        if len(group) == 3 and first + 2 >= len(bits):
+            other = [group[1], group[0], group[2]]
+        rounds.append(list(zip(group, other)))
     return rounds
 
 
@@ -214,8 +218,10 @@
         for w in (gate_weight, up_weight, down_weight)
     )
 
-    def swap(x, rep_xor, exp_xor, tp_xor):
-        return lax.ppermute(x, AXES, partner(mesh_shape, rep_xor, exp_xor, tp_xor))
+    def swap(x, exp_xor, offsets):
+        return lax.ppermute(x, AXES, partner(mesh_shape, exp_xor, offsets))
+
+    stay = ((0, 0), (0, 0))
 
     gathered = pack(tokens, expert_ids, gate_ints)
     rounds = exchange_rounds(mesh_shape)
@@ -231,21 +237,21 @@
         if at < len(shares) - 1:
             load(shares[at])
         gathered = jnp.concatenate(
-            [gathered] + [swap(gathered, r, 0, t) for r, t in offsets], axis=0
+            [gathered] + [swap(gathered, 0, offset) for offset in offsets], axis=0
         )
         if at < len(shares) - 1:
             gathered, loaded[-1] = lax.optimization_barrier((gathered, loaded[-1]))
     load(shares[-1])
-    far = swap(gathered, 0, 1, 0)
+    far = swap(gathered, 1, stay)
     keep, send = run_experts(gathered, far, loaded, gate_weight, up_weight, down_weight)
-    total = keep + swap(send, 0, 1, 0).astype(jnp.float32)
+    total = keep + swap(send, 1, stay).astype(jnp.float32)
     for offsets in reversed(rounds):
         part = total.shape[0] // (len(offsets) + 1)
         pieces = [total[i * part : (i + 1) * part] for i in range(len(offsets) + 1)]
         total = pieces[0]
         moves = list(zip(pieces[1:], offsets))
-        for piece, (r, t) in moves if offsets is rounds[-1] else reversed(moves):
-            total = total + swap(piece.astype(jnp.bfloat16), r, 0, t).astype(jnp.float32)
+        for piece, offset in moves if offsets is rounds[-1] else reversed(moves):
+            total = total + swap(piece.astype(jnp.bfloat16), 0, offset).astype(jnp.float32)
     return total.astype(jnp.bfloat16)
 
 

time: 49.2 us -> 48.7 us (0.990)
  transfers between devices with their start and end apart: 14 -> 14, of which waited for: 8 -> 8; matrix products, arithmetic and copies ran while one was open for 0% -> 0% of each run, Pallas kernels for 21% -> 22%
where the time goes in v5:
time: 48.7 us; the launch traced here: 48.6 us
  Pallas kernels  18.3 us (38%)
  starting transfers between devices  17 us (35%)
  waiting for transfers between devices  12.1 us (25%)
  other arithmetic  0.97 us (2%)
    ppermute x14, starting transfers between devices, swap(): return lax.ppermute(x, AXES, partner(mesh_shape, exp_xor, offsets))  17 us
    ppermute x14, waiting for transfers between devices, swap(): return lax.ppermute(x, AXES, partner(mesh_shape, exp_xor, offsets))  12.1 us
    pallas_call x3, Pallas kernels, load_early(): pl.pallas_call(functools.partial(early_kernel, first), out_shape=(pltpu.V...  10.5 us
    pallas_call x1, Pallas kernels, run_experts(): pl.pallas_call(functools.partial(expert_kernel, len(loaded), late_steps,...  7.05 us
  transfers between devices with their start and end apart: 14, of which 8 were waited for; matrix products, arithmetic and copies ran while one was open for 0% of the time, Pallas kernels for 22%

profile of v5, /device:TPU:0, one launch (start us, length us, event | category | flops | bytes accessed | tf_op | source)
XLA Modules:
  0.0 48.6 jit_solution(17985149879890572188)
XLA Ops:
  0.0 0.8 %shard_map.64.after = bf16[4,4224]{1,0:T(4,128)(2,1)S(1)} custom-call(s32[2,4]{1,0:T(2,128)} %bitcast.2, s32[2,4]{1,0:T(2,128)} %bitcast.3, bf16[4,4096]{1,0:T(4,128)(2,1)} %tokens.1), custom_call_target="tpu_custom_call" | custom-call | tf_op jit(solution)/shard_map/pallas_call | solution.py:66
  0.8 4.1 %collective-permute-start.2 = (bf16[4,4224]{1,0:T(4,128)(2,1)S(1)}, bf16[4,4224]{1,0:T(4,128)(2,1)S(1)}, u32[]{:S(2)}, u32[]{:S(2)}) collective-permute-start(bf16[4,4224]{1,0:T(4,128)(2,1)S(1)} %shard_map.64.after), channel_id=1, source_target_pairs={{0,4},{1,5},{2,6},{3,7},{4,0},{5,1},{6,2},{7,3},{8,12},{9,13},{10,... | collective-permute-start | bytes 101384 | tf_op jit(solution)/shard_map/ppermute | solution.py:222
  4.9 1.6 %collective-permute-start.1 = (bf16[4,4224]{1,0:T(4,128)(2,1)S(1)}, bf16[4,4224]{1,0:T(4,128)(2,1)S(1)}, u32[]{:S(2)}, u32[]{:S(2)}) collective-permute-start(bf16[4,4224]{1,0:T(4,128)(2,1)S(1)} %shard_map.64.after), channel_id=1, source_target_pairs={{0,2},{1,3},{2,0},{3,1},{4,6},{5,7},{6,4},{7,5},{8,10},{9,11},{10,... | collective-permute-start | bytes 101384 | tf_op jit(solution)/shard_map/ppermute | solution.py:222
  6.5 3.7 %shard_map.65 = (bf16[1280,1792]{1,0:T(8,128)(2,1)S(1)}, bf16[1280,1792]{1,0:T(8,128)(2,1)S(1)}) custom-call(bf16[2,4096,1792]{2,1,0:T(8,128)(2,1)} %refs_2_.1, bf16[2,4096,1792]{2,1,0:T(8,128)(2,1)} %refs_3_.1, bf16[4,4224]{1,0:T(4,128)(2,1)S(1)} %shard_map.64.after), custom_call_target="tpu_custom_call" | custom-call | bytes 18350080 | tf_op jit(solution)/shard_map/pallas_call | solution.py:92
  10.2 2.0 %collective-permute-done = bf16[4,4224]{1,0:T(4,128)(2,1)S(1)} collective-permute-done((bf16[4,4224]{1,0:T(4,128)(2,1)S(1)}, bf16[4,4224]{1,0:T(4,128)(2,1)S(1)}, u32[]{:S(2)}, u32[]{:S(2)}) %collective-permute-start) | collective-permute-done | bytes 33824 | tf_op jit(solution)/shard_map/ppermute | solution.py:222
  12.3 2.5 %collective-permute-start.5 = (bf16[16,4224]{1,0:T(8,128)(2,1)S(1)}, bf16[16,4224]{1,0:T(8,128)(2,1)S(1)}, u32[]{:S(2)}, u32[]{:S(2)}) collective-permute-start(bf16[16,4224]{1,0:T(8,128)(2,1)S(1)} %pad_maximum_fusion.1.after), channel_id=1, source_target_pairs={{0,17},{1,16},{2,19},{3,18},{4,21},{5,20},{6,23},{7,22},{8,25},{9,... | collective-permute-start | bytes 405512 | tf_op jit(solution)/shard_map/ppermute | solution.py:222
  14.8 0.5 %collective-permute-start.4 = (bf16[16,4224]{1,0:T(8,128)(2,1)S(1)}, bf16[16,4224]{1,0:T(8,128)(2,1)S(1)}, u32[]{:S(2)}, u32[]{:S(2)}) collective-permute-start(bf16[16,4224]{1,0:T(8,128)(2,1)S(1)} %pad_maximum_fusion.1.after), channel_id=1, source_target_pairs={{0,16},{1,17},{2,18},{3,19},{4,20},{5,21},{6,22},{7,23},{8,9},{9,8... | collective-permute-start | bytes 405512 | tf_op jit(solution)/shard_map/ppermute | solution.py:222
  15.3 0.5 %collective-permute-start.3 = (bf16[16,4224]{1,0:T(8,128)(2,1)S(1)}, bf16[16,4224]{1,0:T(8,128)(2,1)S(1)}, u32[]{:S(2)}, u32[]{:S(2)}) collective-permute-start(bf16[16,4224]{1,0:T(8,128)(2,1)S(1)} %pad_maximum_fusion.1.after), channel_id=1, source_target_pairs={{0,1},{1,0},{2,3},{3,2},{4,5},{5,4},{6,7},{7,6},{8,24},{9,25},{10,... | collective-permute-start | bytes 405512 | tf_op jit(solution)/shard_map/ppermute | solution.py:222
  15.8 4.7 %shard_map.66 = (bf16[1792,1792]{1,0:T(8,128)(2,1)S(1)}, bf16[1792,1792]{1,0:T(8,128)(2,1)S(1)}) custom-call(bf16[2,4096,1792]{2,1,0:T(8,128)(2,1)} %refs_2_.1, bf16[2,4096,1792]{2,1,0:T(8,128)(2,1)} %refs_3_.1, bf16[16,4224]{1,0:T(8,128)(2,1)S(1)} %pad_maximum_fusion.1.after), custom_call_target="tpu_custom_call" | custom-call | bytes 25690112 | tf_op jit(solution)/shard_map/pallas_call | solution.py:92
  20.9 2.1 %shard_map.67 = (bf16[512,1792]{1,0:T(8,128)(2,1)S(1)}, bf16[512,1792]{1,0:T(8,128)(2,1)S(1)}) custom-call(bf16[2,4096,1792]{2,1,0:T(8,128)(2,1)} %refs_2_.1, bf16[2,4096,1792]{2,1,0:T(8,128)(2,1)} %refs_3_.1, bf16[64,4224]{1,0:T(8,128)(2,1)S(1)} %pad_maximum_fusion.after.refs_0_), custom_call_target="tpu_custom_call" | custom-call | bytes 7340032 | tf_op jit(solution)/shard_map/pallas_call | solution.py:92
  23.0 7.0 %shard_map.68 = (f32[64,4096]{1,0:T(8,128)S(1)}, bf16[64,4096]{1,0:T(8,128)(2,1)S(1)}) custom-call(bf16[64,4224]{1,0:T(8,128)(2,1)S(1)} %pad_maximum_fusion.after.refs_0_, bf16[64,4224]{1,0:T(8,128)(2,1)S(1)} %collective-permute-done.6.refs_1_, bf16[2,4096,1792]{2,1,0:T(8,128)(2,1)} %refs_2_.1, bf16[2,4096,1792]{2,1,0:T(8,128)(2,1)} %refs_3_.1, ...), custom_call_target="tpu_custom_call" | custom-call | tf_op jit(solution)/shard_map/pallas_call | solution.py:191
  30.0 0.6 %collective-permute-start.7 = (bf16[64,4096]{1,0:T(8,128)(2,1)S(1)}, bf16[64,4096]{1,0:T(8,128)(2,1)S(1)}, u32[]{:S(2)}, u32[]{:S(2)}) collective-permute-start(bf16[64,4096]{1,0:T(8,128)(2,1)S(1)} %get-tuple-element.32), channel_id=1, source_target_pairs={{0,8},{1,9},{2,10},{3,11},{4,12},{5,13},{6,14},{7,15},{8,0},{9,1},... | collective-permute-start | bytes 1572872 | tf_op jit(solution)/shard_map/ppermute | solution.py:222
  30.6 1.5 %collective-permute-done.7 = bf16[64,4096]{1,0:T(8,128)(2,1)S(1)} collective-permute-done((bf16[64,4096]{1,0:T(8,128)(2,1)S(1)}, bf16[64,4096]{1,0:T(8,128)(2,1)S(1)}, u32[]{:S(2)}, u32[]{:S(2)}) %collective-permute-start.7) | collective-permute-done | bytes 524320 | tf_op jit(solution)/shard_map/ppermute | solution.py:222
  32.3 1.4 %collective-permute-start.8 = (bf16[16,4096]{1,0:T(8,128)(2,1)S(1)}, bf16[16,4096]{1,0:T(8,128)(2,1)S(1)}, u32[]{:S(2)}, u32[]{:S(2)}) collective-permute-start(bf16[16,4096]{1,0:T(8,128)(2,1)S(1)} %get-tuple-element.37), channel_id=1, source_target_pairs={{0,1},{1,0},{2,3},{3,2},{4,5},{5,4},{6,7},{7,6},{8,24},{9,25},{10,... | collective-permute-start | bytes 393224 | tf_op jit(solution)/shard_map/ppermute | solution.py:222
  33.7 1.4 %collective-permute-start.10 = (bf16[16,4096]{1,0:T(8,128)(2,1)S(1)}, bf16[16,4096]{1,0:T(8,128)(2,1)S(1)}, u32[]{:S(2)}, u32[]{:S(2)}) collective-permute-start(bf16[16,4096]{1,0:T(8,128)(2,1)S(1)} %get-tuple-element.38), channel_id=1, source_target_pairs={{0,17},{1,16},{2,19},{3,18},{4,21},{5,20},{6,23},{7,22},{8,25},{9,... | collective-permute-start | bytes 393224 | tf_op jit(solution)/shard_map/ppermute | solution.py:222
  35.1 0.7 %collective-permute-start.9 = (bf16[16,4096]{1,0:T(8,128)(2,1)S(1)}, bf16[16,4096]{1,0:T(8,128)(2,1)S(1)}, u32[]{:S(2)}, u32[]{:S(2)}) collective-permute-start(bf16[16,4096]{1,0:T(8,128)(2,1)S(1)} %get-tuple-element.39), channel_id=1, source_target_pairs={{0,16},{1,17},{2,18},{3,19},{4,20},{5,21},{6,22},{7,23},{8,9},{9,8... | collective-permute-start | bytes 393224 | tf_op jit(solution)/shard_map/ppermute | solution.py:222
  35.8 1.5 %collective-permute-done.8 = bf16[16,4096]{1,0:T(8,128)(2,1)S(1)} collective-permute-done((bf16[16,4096]{1,0:T(8,128)(2,1)S(1)}, bf16[16,4096]{1,0:T(8,128)(2,1)S(1)}, u32[]{:S(2)}, u32[]{:S(2)}) %collective-permute-start.8) | collective-permute-done | bytes 131104 | tf_op jit(solution)/shard_map/ppermute | solution.py:222
  37.3 3.1 %collective-permute-done.10 = bf16[16,4096]{1,0:T(8,128)(2,1)S(1)} collective-permute-done((bf16[16,4096]{1,0:T(8,128)(2,1)S(1)}, bf16[16,4096]{1,0:T(8,128)(2,1)S(1)}, u32[]{:S(2)}, u32[]{:S(2)}) %collective-permute-start.10) | collective-permute-done | bytes 131104 | tf_op jit(solution)/shard_map/ppermute | solution.py:222
  40.4 1.2 %collective-permute-done.9 = bf16[16,4096]{1,0:T(8,128)(2,1)S(1)} collective-permute-done((bf16[16,4096]{1,0:T(8,128)(2,1)S(1)}, bf16[16,4096]{1,0:T(8,128)(2,1)S(1)}, u32[]{:S(2)}, u32[]{:S(2)}) %collective-permute-start.9) | collective-permute-done | bytes 131104 | tf_op jit(solution)/shard_map/ppermute | solution.py:222
  41.8 1.9 %collective-permute-start.13 = (bf16[4,4096]{1,0:T(4,128)(2,1)S(1)}, bf16[4,4096]{1,0:T(4,128)(2,1)S(1)}, u32[]{:S(2)}, u32[]{:S(2)}) collective-permute-start(bf16[4,4096]{1,0:T(4,128)(2,1)S(1)} %get-tuple-element.41), channel_id=1, source_target_pairs={{0,6},{1,7},{2,4},{3,5},{4,2},{5,3},{6,0},{7,1},{8,14},{9,15},{10,... | collective-permute-start | bytes 98312 | tf_op jit(solution)/shard_map/ppermute | solution.py:222
  43.7 1.6 %collective-permute-start.12 = (bf16[4,4096]{1,0:T(4,128)(2,1)S(1)}, bf16[4,4096]{1,0:T(4,128)(2,1)S(1)}, u32[]{:S(2)}, u32[]{:S(2)}) collective-permute-start(bf16[4,4096]{1,0:T(4,128)(2,1)S(1)} %get-tuple-element.42), channel_id=1, source_target_pairs={{0,2},{1,3},{2,0},{3,1},{4,6},{5,7},{6,4},{7,5},{8,10},{9,11},{10,... | collective-permute-start | bytes 98312 | tf_op jit(solution)/shard_map/ppermute | solution.py:222
  45.2 1.9 %collective-permute-done.11 = bf16[4,4096]{1,0:T(4,128)(2,1)S(1)} collective-permute-done((bf16[4,4096]{1,0:T(4,128)(2,1)S(1)}, bf16[4,4096]{1,0:T(4,128)(2,1)S(1)}, u32[]{:S(2)}, u32[]{:S(2)}) %collective-permute-start.11) | collective-permute-done | bytes 32800 | tf_op jit(solution)/shard_map/ppermute | solution.py:222
  47.1 0.8 %collective-permute-done.13 = bf16[4,4096]{1,0:T(4,128)(2,1)S(1)} collective-permute-done((bf16[4,4096]{1,0:T(4,128)(2,1)S(1)}, bf16[4,4096]{1,0:T(4,128)(2,1)S(1)}, u32[]{:S(2)}, u32[]{:S(2)}) %collective-permute-start.13) | collective-permute-done | bytes 32800 | tf_op jit(solution)/shard_map/ppermute | solution.py:222
  47.9 0.6 %fusion.4 = bf16[4,4096]{1,0:T(4,128)(2,1)} fusion(f32[16,4096]{1,0:T(8,128)S(1)} %get-tuple-element.34, bf16[4,4096]{1,0:T(4,128)(2,1)S(1)} %collective-permute-done.13, bf16[4,4096]{1,0:T(4,128)(2,1)S(1)} %collective-permute-done.12, bf16[4,4096]{1,0:T(4,128)(2,1)S(1)} %collective-permute-done.11), kind=kLoop, calls=%fused_computation.9 | loop fusion | flops 114688 | bytes 196608 | tf_op jit(solution)/shard_map/convert_element_type | solution.py:255
  (16 shorter events, 0.8 us)
Async XLA Ops:
  0.8 9.4 %collective-permute-start.2 = (bf16[4,4224]{1,0:T(4,128)(2,1)S(1)}, bf16[4,4224]{1,0:T(4,128)(2,1)S(1)}, u32[]{:S(2)}, u32[]{:S(2)}) collective-permute-start(bf16[4,4224]{1,0:T(4,128)(2,1)S(1)} %shard_map.64.after), channel_id=1, source_target_pairs={{0,4},{1,5},{2,6},{3,7},{4,0},{5,1},{6,2},{7,3},{8,12},{9,13},{10,... | collective-permute-start | bytes 101384 | tf_op jit(solution)/shard_map/ppermute | solution.py:222
  4.9 5.3 %collective-permute-start.1 = (bf16[4,4224]{1,0:T(4,128)(2,1)S(1)}, bf16[4,4224]{1,0:T(4,128)(2,1)S(1)}, u32[]{:S(2)}, u32[]{:S(2)}) collective-permute-start(bf16[4,4224]{1,0:T(4,128)(2,1)S(1)} %shard_map.64.after), channel_id=1, source_target_pairs={{0,2},{1,3},{2,0},{3,1},{4,6},{5,7},{6,4},{7,5},{8,10},{9,11},{10,... | collective-permute-start | bytes 101384 | tf_op jit(solution)/shard_map/ppermute | solution.py:222
  6.5 5.7 %collective-permute-start = (bf16[4,4224]{1,0:T(4,128)(2,1)S(1)}, bf16[4,4224]{1,0:T(4,128)(2,1)S(1)}, u32[]{:S(2)}, u32[]{:S(2)}) collective-permute-start(bf16[4,4224]{1,0:T(4,128)(2,1)S(1)} %shard_map.64.after), channel_id=1, source_target_pairs={{0,6},{1,7},{2,4},{3,5},{4,2},{5,3},{6,0},{7,1},{8,14},{9,15},{10,... | collective-permute-start | bytes 101384 | tf_op jit(solution)/shard_map/ppermute | solution.py:222
  12.3 8.3 %collective-permute-start.5 = (bf16[16,4224]{1,0:T(8,128)(2,1)S(1)}, bf16[16,4224]{1,0:T(8,128)(2,1)S(1)}, u32[]{:S(2)}, u32[]{:S(2)}) collective-permute-start(bf16[16,4224]{1,0:T(8,128)(2,1)S(1)} %pad_maximum_fusion.1.after), channel_id=1, source_target_pairs={{0,17},{1,16},{2,19},{3,18},{4,21},{5,20},{6,23},{7,22},{8,25},{9,... | collective-permute-start | bytes 405512 | tf_op jit(solution)/shard_map/ppermute | solution.py:222
  14.8 5.8 %collective-permute-start.4 = (bf16[16,4224]{1,0:T(8,128)(2,1)S(1)}, bf16[16,4224]{1,0:T(8,128)(2,1)S(1)}, u32[]{:S(2)}, u32[]{:S(2)}) collective-permute-start(bf16[16,4224]{1,0:T(8,128)(2,1)S(1)} %pad_maximum_fusion.1.after), channel_id=1, source_target_pairs={{0,16},{1,17},{2,18},{3,19},{4,20},{5,21},{6,22},{7,23},{8,9},{9,8... | collective-permute-start | bytes 405512 | tf_op jit(solution)/shard_map/ppermute | solution.py:222
  15.3 5.4 %collective-permute-start.3 = (bf16[16,4224]{1,0:T(8,128)(2,1)S(1)}, bf16[16,4224]{1,0:T(8,128)(2,1)S(1)}, u32[]{:S(2)}, u32[]{:S(2)}) collective-permute-start(bf16[16,4224]{1,0:T(8,128)(2,1)S(1)} %pad_maximum_fusion.1.after), channel_id=1, source_target_pairs={{0,1},{1,0},{2,3},{3,2},{4,5},{5,4},{6,7},{7,6},{8,24},{9,25},{10,... | collective-permute-start | bytes 405512 | tf_op jit(solution)/shard_map/ppermute | solution.py:222
  20.8 2.2 %collective-permute-start.6 = (bf16[64,4224]{1,0:T(8,128)(2,1)S(1)}, bf16[64,4224]{1,0:T(8,128)(2,1)S(1)}, u32[]{:S(2)}, u32[]{:S(2)}) collective-permute-start(bf16[64,4224]{1,0:T(8,128)(2,1)S(1)} %pad_maximum_fusion.after.refs_0_), channel_id=1, source_target_pairs={{0,8},{1,9},{2,10},{3,11},{4,12},{5,13},{6,14},{7,15},{8,0},{9,1},... | collective-permute-start | bytes 1622024 | tf_op jit(solution)/shard_map/ppermute | solution.py:222
  30.0 2.1 %collective-permute-start.7 = (bf16[64,4096]{1,0:T(8,128)(2,1)S(1)}, bf16[64,4096]{1,0:T(8,128)(2,1)S(1)}, u32[]{:S(2)}, u32[]{:S(2)}) collective-permute-start(bf16[64,4096]{1,0:T(8,128)(2,1)S(1)} %get-tuple-element.32), channel_id=1, source_target_pairs={{0,8},{1,9},{2,10},{3,11},{4,12},{5,13},{6,14},{7,15},{8,0},{9,1},... | collective-permute-start | bytes 1572872 | tf_op jit(solution)/shard_map/ppermute | solution.py:222
  32.3 5.0 %collective-permute-start.8 = (bf16[16,4096]{1,0:T(8,128)(2,1)S(1)}, bf16[16,4096]{1,0:T(8,128)(2,1)S(1)}, u32[]{:S(2)}, u32[]{:S(2)}) collective-permute-start(bf16[16,4096]{1,0:T(8,128)(2,1)S(1)} %get-tuple-element.37), channel_id=1, source_target_pairs={{0,1},{1,0},{2,3},{3,2},{4,5},{5,4},{6,7},{7,6},{8,24},{9,25},{10,... | collective-permute-start | bytes 393224 | tf_op jit(solution)/shard_map/ppermute | solution.py:222
  33.7 6.7 %collective-permute-start.10 = (bf16[16,4096]{1,0:T(8,128)(2,1)S(1)}, bf16[16,4096]{1,0:T(8,128)(2,1)S(1)}, u32[]{:S(2)}, u32[]{:S(2)}) collective-permute-start(bf16[16,4096]{1,0:T(8,128)(2,1)S(1)} %get-tuple-element.38), channel_id=1, source_target_pairs={{0,17},{1,16},{2,19},{3,18},{4,21},{5,20},{6,23},{7,22},{8,25},{9,... | collective-permute-start | bytes 393224 | tf_op jit(solution)/shard_map/ppermute | solution.py:222
  35.1 6.4 %collective-permute-start.9 = (bf16[16,4096]{1,0:T(8,128)(2,1)S(1)}, bf16[16,4096]{1,0:T(8,128)(2,1)S(1)}, u32[]{:S(2)}, u32[]{:S(2)}) collective-permute-start(bf16[16,4096]{1,0:T(8,128)(2,1)S(1)} %get-tuple-element.39), channel_id=1, source_target_pairs={{0,16},{1,17},{2,18},{3,19},{4,20},{5,21},{6,22},{7,23},{8,9},{9,8... | collective-permute-start | bytes 393224 | tf_op jit(solution)/shard_map/ppermute | solution.py:222
  41.7 5.4 %collective-permute-start.11 = (bf16[4,4096]{1,0:T(4,128)(2,1)S(1)}, bf16[4,4096]{1,0:T(4,128)(2,1)S(1)}, u32[]{:S(2)}, u32[]{:S(2)}) collective-permute-start(bf16[4,4096]{1,0:T(4,128)(2,1)S(1)} %get-tuple-element.40), channel_id=1, source_target_pairs={{0,4},{1,5},{2,6},{3,7},{4,0},{5,1},{6,2},{7,3},{8,12},{9,13},{10,... | collective-permute-start | bytes 98312 | tf_op jit(solution)/shard_map/ppermute | solution.py:222
  41.8 6.1 %collective-permute-start.13 = (bf16[4,4096]{1,0:T(4,128)(2,1)S(1)}, bf16[4,4096]{1,0:T(4,128)(2,1)S(1)}, u32[]{:S(2)}, u32[]{:S(2)}) collective-permute-start(bf16[4,4096]{1,0:T(4,128)(2,1)S(1)} %get-tuple-element.41), channel_id=1, source_target_pairs={{0,6},{1,7},{2,4},{3,5},{4,2},{5,3},{6,0},{7,1},{8,14},{9,15},{10,... | collective-permute-start | bytes 98312 | tf_op jit(solution)/shard_map/ppermute | solution.py:222
  43.7 4.2 %collective-permute-start.12 = (bf16[4,4096]{1,0:T(4,128)(2,1)S(1)}, bf16[4,4096]{1,0:T(4,128)(2,1)S(1)}, u32[]{:S(2)}, u32[]{:S(2)}) collective-permute-start(bf16[4,4096]{1,0:T(4,128)(2,1)S(1)} %get-tuple-element.42), channel_id=1, source_target_pairs={{0,2},{1,3},{2,0},{3,1},{4,6},{5,7},{6,4},{7,5},{8,10},{9,11},{10,... | collective-permute-start | bytes 98312 | tf_op jit(solution)/shard_map/ppermute | solution.py:222
